TPU v7x, 32 devices: a whole 2x2x4 slice. The times are simulated.
32 devices in a mesh: prow: 4 (over y, core), pcol: 8 (over z, x).
Axes of the slice: x: 2, y: 2, z: 4, core: 2. Of those that a mesh axis runs over, the one named last changes fastest.
Arguments:
- diag_one: float32 [1024, 1024], P('pcol')
- top_rows: bfloat16 [1024, 1024], P('pcol'), may hold values from -0.1875 to 0.1875
- panel_one: bfloat16 [16384, 1024], P(('prow', 'pcol')), may hold values from -6 to 6
- first_block: int32 [64], P(('prow', 'pcol')), may hold values from 0 to 3
- target: int32 [64], P(('prow', 'pcol')), may hold values from 0 to 63, as said below
- diag_two: float32 [1024, 1024], P('pcol'), may hold values from -6 to 6
- panel_two: bfloat16 [16384, 1024], P(('prow', 'pcol')), may hold values from -6 to 6
Outputs:
- panel_factor: bfloat16 [16384, 1024], P(('prow', 'pcol'))
- top_factor: bfloat16 [1024, 1024], P('pcol')
- diag_next: float32 [1024, 1024], P('pcol')
- panel_next: float32 [16384, 1024], P(('prow', 'pcol'))
Inputs may be any that keep to these rules, and one draw needn't show every extreme that they name: Row block t of the second supernode is held by grid row (t // 2) // 8 and grid column (t // 2) % 8; target[i] lies in the grid column of row block i; the 2 row blocks of one device go to 2 different grid rows; in every grid column one grid row receives a row block from every grid row.
All inputs are finite; a program needn't handle non-finite values.
Results may differ from a plain program's by a relative error of at most 0.0021.
Values may be sent and summed in bfloat16 or wider, within the bound.
No kernel may reach another device: no remote copies, remote signals or barrier semaphores. Data moves between devices by JAX's collectives and lax.ppermute only.
A program may use at most 128 MiB of HBM per device.

v0:
```python
import functools

import jax
import jax.numpy as jnp
from jax import lax
from jax.experimental import pallas as pl
from jax.experimental.pallas import tpu as pltpu
from jax.sharding import PartitionSpec as P

NB = 128
SUB = 32
VMEM = pl.BlockSpec(memory_space=pltpu.VMEM)
ANY = pl.BlockSpec(memory_space=pl.ANY)
SMEM = pl.BlockSpec(memory_space=pltpu.SMEM)


def split3(x):
    hi = x.astype(jnp.bfloat16)
    rest = x - hi.astype(jnp.float32)
    mid = rest.astype(jnp.bfloat16)
    low = (rest - mid.astype(jnp.float32)).astype(jnp.bfloat16)
    return hi, mid, low


def left_terms(x):
    hi, mid, low = split3(x)
    return jnp.concatenate([hi, hi, mid], 0)


def right_terms(x):
    hi, mid, low = split3(x)
    return jnp.concatenate([hi, mid, hi], 0)


def dot_tn(left, right):
    return lax.dot_general(
        left, right, (((0,), (0,)), ((), ())), preferred_element_type=jnp.float32
    )


def dot_nt(left, right):
    return lax.dot_general(
        left, right, (((1,), (1,)), ((), ())), preferred_element_type=jnp.float32
    )


def lanes(x, column):
    return jnp.broadcast_to(x[:, column : column + 1], (8, NB))


def sublanes(x, i):
    return jnp.broadcast_to(x[i : i + 1, :], x.shape)


def wide(x, width):
    return jnp.tile(x, (1, width // x.shape[1]))


def eliminate(rows, base):
    width = rows[0].shape[1]
    groups = len(rows)
    rows = list(rows)
    done = []
    sublane = lax.broadcasted_iota(jnp.int32, (8, NB), 0)

    def columns(q):
        return [
            {p: lanes(rows[p], base + 8 * q + c) for p in range(q, groups)} for c in range(8)
        ]

    now = columns(0)
    for q in range(groups):
        later = columns(q + 1) if q + 1 < groups else []
        pivots = None
        for j in range(8):
            pivot = sublanes(now[j][q], j)
            pivots = pivot if pivots is None else jnp.where(sublane == j, pivot, pivots)
            inverse = 1.0 / pivot
            ratio = {p: now[j][p] * inverse for p in range(q, groups)}
            for c in range(j + 1, 8):
                entry = sublanes(now[j][q], c)
                for p in range(q, groups):
                    now[c][p] = now[c][p] - ratio[p] * entry
            for c in range(len(later)):
                entry = sublanes(now[j][q + 1], c)
                for p in range(q + 1, groups):
                    later[c][p] = later[c][p] - ratio[p] * entry
            row = sublanes(rows[q], j)
            if j < 7:
                below = jnp.where(sublane > j, ratio[q], 0.0)
                rows[q] = rows[q] - wide(below, width) * row
            for p in range(q + 1, groups):
                rows[p] = rows[p] - wide(ratio[p], width) * row
        done.append(rows[q] * wide(lax.rsqrt(pivots), width))
        now = later
    return done


def factor_block(block):
    rows = [block[8 * i : 8 * i + 8] for i in range(NB // 8)]
    step = SUB // 8
    done = []
    for b in range(NB // SUB):
        part = eliminate(rows[b * step : (b + 1) * step], b * SUB)
        done += part
        if (b + 1) * SUB < NB:
            solved = jnp.concatenate(part, 0)
            change = dot_tn(left_terms(solved[:, (b + 1) * SUB : NB]), right_terms(solved))
            for p in range((b + 1) * step, NB // 8):
                k = p - (b + 1) * step
                rows[p] = rows[p] - change[8 * k : 8 * k + 8]
    return jnp.concatenate(done, 0)


def assemble_pieces(place_ref, pieces, work, sems):
    half, width = pieces[0].shape
    count = work.shape[0] // NB
    column, place = place_ref[0], place_ref[1] % 2
    copies = []
    for i, ref in enumerate(pieces):
        core, crossed, turn = i // count, i // (count // 2) % 2, i % (count // 2)
        strip = column ^ (2 * turn + crossed)
        row = pl.multiple_of(strip * NB + (place ^ core) * half, half)
        for d in range(width // NB):
            lane = pl.multiple_of(((strip + d) % count) * NB, NB)
            copies.append(
                pltpu.make_async_copy(
                    ref.at[:, d * NB : (d + 1) * NB],
                    work.at[pl.ds(row, half), pl.ds(lane, NB)],
                    sems.at[len(copies)],
                )
            )
    for copy in copies:
        copy.start()
    for copy in copies:
        copy.wait()
    for i in range(count):
        for j in range(i + width // NB, count):
            here, there = slice(i * NB, (i + 1) * NB), slice(j * NB, (j + 1) * NB)
            work[here, there] = work[there, here].T


def factor_pieces_kernel(pieces, place_ref, *refs):
    *rest, sems = refs[pieces:]
    assemble_pieces(place_ref, refs[:pieces], rest[4], sems)
    factor_kernel(*rest)


def factor_whole_kernel(diag_ref, *refs):
    *rest, _ = refs
    rest[4][...] = diag_ref[...]
    factor_kernel(*rest)


def factor_kernel(own_ref, hi_ref, lo_ref, own_out, work, block, left, right):
    size = work.shape[0]
    count = size // NB
    same = lax.broadcasted_iota(jnp.int32, (NB, NB), 0) == lax.broadcasted_iota(
        jnp.int32, (NB, NB), 1
    )
    unit = same.astype(jnp.float32)

    def strip(k, to=None):
        return slice(k * NB, (k + 1 if to is None else to) * NB)

    def solve(k, inverse, columns):
        solved = dot_tn(inverse, right_terms(work[strip(k), columns]))
        work[strip(k), columns] = solved
        left[k % 2, :, columns] = left_terms(solved)
        right[k % 2, :, columns] = right_terms(solved)

    def update(i, k, columns):
        work[strip(i), columns] = work[strip(i), columns] - dot_tn(
            left[k % 2, :, strip(i)], right[k % 2, :, columns]
        )

    def rest(k, inverse, plain):
        if k + 2 < count:
            solve(k, inverse, strip(k + 2, count))
        if k:
            solve(k, inverse, strip(0, k))
        work[strip(k), strip(k)] = plain
        right[k % 2, :, strip(k)] = right_terms(plain)
        upto = (k + 1) * NB
        value = work[strip(k), :upto]
        hi = value.astype(jnp.bfloat16)
        lo = (value - hi.astype(jnp.float32)).astype(jnp.bfloat16)
        hi_ref[strip(k), :upto] = hi
        lo_ref[strip(k), :upto] = lo
        if upto < size:
            hi_ref[strip(k), upto:] = jnp.zeros((NB, size - upto), jnp.bfloat16)
            lo_ref[strip(k), upto:] = jnp.zeros((NB, size - upto), jnp.bfloat16)
        rows = own_ref[:, :upto]
        own_out[:, strip(k)] = (dot_nt(rows, hi) + dot_nt(rows, lo)).astype(jnp.bfloat16)
        for i in range(k + 1, count):
            first = i + 1 if i == k + 1 else i
            if first < count:
                update(i, k, strip(first, count))
            work[strip(i), strip(k)] = jnp.zeros((NB, NB), jnp.float32)
            update(i, k, strip(0, k + 1))

    pending = None
    for k in range(count):
        block[k % 2, :, :NB] = work[strip(k), strip(k)]
        block[k % 2, :, NB:] = unit
        block[k % 2] = factor_block(block[k % 2])
        if pending is not None:
            rest(*pending)
        plain = block[k % 2, :, NB:]
        inverse = left_terms(plain.T)
        if k + 1 < count:
            solve(k, inverse, strip(k + 1))
            update(k + 1, k, strip(k + 1))
        pending = (k, inverse, plain)
    rest(*pending)


def inverse_factor(kernel, in_specs, size, operands):
    half = jax.ShapeDtypeStruct((size, size), jnp.bfloat16)
    return pl.pallas_call(
        kernel,
        out_shape=(half, half, jax.ShapeDtypeStruct(operands[-1].shape, jnp.bfloat16)),
        in_specs=in_specs,
        out_specs=(VMEM,) * 3,
        scratch_shapes=[
            pltpu.VMEM((size, size), jnp.float32),
            pltpu.VMEM((2, NB, 2 * NB), jnp.float32),
            pltpu.VMEM((2, 3 * NB, size), jnp.bfloat16),
            pltpu.VMEM((2, 3 * NB, size), jnp.bfloat16),
            pltpu.SemaphoreType.DMA((80,)),
        ],
        compiler_params=pltpu.CompilerParams(vmem_limit_bytes=20 * 2**20),
        cost_estimate=pl.CostEstimate(
            flops=40 * size**3, bytes_accessed=8 * size * size, transcendentals=0
        ),
        name="inverse_factor",
    )(*operands)


def shifted(x, axis, s):
    return lax.ppermute(x, axis, [(i, i ^ s) for i in range(lax.axis_size(axis))])


def cut_piece(strip):
    rows, size = strip.shape
    core = lax.axis_index("prow") % 2
    piece = lax.dynamic_slice_in_dim(strip, core * (rows // 2), rows // 2, 0)
    return lax.dynamic_slice_in_dim(
        jnp.concatenate([piece, piece], 1), lax.axis_index("pcol") * rows, size // 2 + rows, 1
    )


def factor_pieces(place, size, mine, own):
    pieces = mine + [shifted(part, "prow", 1) for part in mine]
    return inverse_factor(
        functools.partial(factor_pieces_kernel, len(pieces)),
        [SMEM] + [ANY] * len(pieces) + [VMEM],
        size,
        (place, *pieces, own),
    )


def solve_rows(x, hi_ref, lo_ref):
    size = hi_ref.shape[0]
    width = 256
    parts = []
    for j in range(size // width):
        rows, upto = slice(j * width, (j + 1) * width), (j + 1) * width
        parts.append(
            dot_nt(x[:, :upto], hi_ref[rows, :upto]) + dot_nt(x[:, :upto], lo_ref[rows, :upto])
        )
    return jnp.concatenate(parts, 1).astype(jnp.bfloat16)


def top_kernel(hi_ref, lo_ref, first_ref, second_ref, out_ref):
    rows = first_ref.shape[0]
    for c, ref in enumerate((first_ref, second_ref)):
        out_ref[c * rows : (c + 1) * rows, :] = solve_rows(ref[...], hi_ref, lo_ref)


def solve_top(hi, lo, first, second):
    size = hi.shape[0]
    rows = 2 * first.shape[0]
    return pl.pallas_call(
        top_kernel,
        out_shape=jax.ShapeDtypeStruct((rows, size), jnp.bfloat16),
        in_specs=[VMEM] * 4,
        out_specs=VMEM,
        compiler_params=pltpu.CompilerParams(vmem_limit_bytes=12 * 2**20),
        cost_estimate=pl.CostEstimate(
            flops=3 * size * size * rows, bytes_accessed=8 * size * size, transcendentals=0
        ),
        name="solve_top",
    )(hi, lo, first, second)


def route_kernel(
    block_rows, grid_cols, place_ref, first_ref, target_ref, panel_ref, _, *outs
):
    own_ref, zeros_ref, *sent_refs = outs
    blocks = first_ref.shape[0]
    size = panel_ref.shape[1]
    row = place_ref[1]
    zeros_ref[...] = jnp.zeros_like(zeros_ref)
    column_block = lax.broadcasted_iota(jnp.int32, (block_rows, size), 1) // block_rows
    for r in range(blocks):
        rows = slice(r * block_rows, (r + 1) * block_rows)
        value = panel_ref[rows, :]
        own_ref[rows, :] = jnp.where(
            column_block >= first_ref[r], value, jnp.zeros_like(value)
        )
    length = block_rows + 16
    sent = []
    for ref in sent_refs:
        sent += [ref.at[i : i + length] for i in range(0, ref.shape[0], length)]
    for s, ref in enumerate(sent):
        ref[...] = jnp.zeros_like(ref)
        for r in range(blocks):
            dest_row = target_ref[r] // (blocks * grid_cols)

            @pl.when(dest_row == row ^ s)
            def _():
                ref[:block_rows, :] = own_ref[r * block_rows : (r + 1) * block_rows, :]
                ref[block_rows:, :] = jnp.full(
                    (16, size), (target_ref[r] % blocks).astype(jnp.float32)
                ).astype(jnp.bfloat16)


def route(place, first_block, target, panel, earlier):
    blocks = first_block.shape[0]
    rows, size = panel.shape
    block_rows = rows // blocks
    grid_rows, grid_cols = lax.axis_size("prow"), lax.axis_size("pcol")
    sent = (1, 1) + (2,) * (grid_rows // 2 - 1)
    own, zeros, *sent = pl.pallas_call(
        functools.partial(route_kernel, block_rows, grid_cols),
        out_shape=(
            jax.ShapeDtypeStruct(panel.shape, jnp.bfloat16),
            jax.ShapeDtypeStruct((NB // 2, size // 2 + NB), jnp.float32),
        )
        + tuple(
            jax.ShapeDtypeStruct((n * (block_rows + 16), size), jnp.bfloat16) for n in sent
        ),
        in_specs=[SMEM] * 3 + [VMEM, ANY],
        out_specs=(VMEM,) * (2 + len(sent)),
        compiler_params=pltpu.CompilerParams(vmem_limit_bytes=12 * 2**20),
        cost_estimate=pl.CostEstimate(
            flops=0, bytes_accessed=2 * (grid_rows + 4) * rows * size, transcendentals=0
        ),
        name="route_panel",
    )(place, first_block, target, panel, earlier)
    return own, zeros, sent


def hold_kernel(x_ref, _, out_ref):
    out_ref[...] = x_ref[...]


def hold(x, earlier):
    return pl.pallas_call(
        hold_kernel,
        out_shape=jax.ShapeDtypeStruct(x.shape, x.dtype),
        in_specs=[VMEM, ANY],
        out_specs=VMEM,
        compiler_params=pltpu.CompilerParams(vmem_limit_bytes=4 * 2**20),
        cost_estimate=pl.CostEstimate(
            flops=0, bytes_accessed=8 * x.size, transcendentals=0
        ),
        name="hold_piece",
    )(x, earlier)


def doubled(held, s):
    return jnp.concatenate([held, shifted(held, "pcol", s)], 0)


def update_kernel(block_rows, place_ref, hi_ref, lo_ref, mine_ref, other_ref, *refs):
    incoming = refs[:-6]
    diag_ref, panel_ref, top_out, diag_out, panel_out, top_all = refs[-6:]
    local = top_out.shape[0]
    half = local // 2
    strips = mine_ref.shape[0] // half
    bits = strips.bit_length() - 1
    column, core = place_ref[0], place_ref[1] % 2
    for c, ref in enumerate((mine_ref, other_ref)):
        for slot in range(strips):
            strip = column ^ sum(((slot >> b) & 1) << (bits - 1 - b) for b in range(bits))
            row = pl.multiple_of(strip * local + (core ^ c) * half, half)
            top_all[pl.ds(row, half), :] = ref[slot * half : (slot + 1) * half, :]
    mine = top_all[pl.ds(pl.multiple_of(column * local, local), local), :]
    top_out[...] = mine
    diag_out[...] = diag_ref[...] - dot_nt(mine, top_all[...])
    panel_out[...] = panel_ref[...].astype(jnp.float32)
    for ref in incoming:
        solved = solve_rows(ref[:block_rows, :], hi_ref, lo_ref)
        change = dot_nt(solved, top_all[...])
        slot = jnp.max(ref[block_rows : block_rows + 16, :NB].astype(jnp.float32))
        there = pl.ds(
            pl.multiple_of(slot.astype(jnp.int32) * block_rows, block_rows), block_rows
        )
        panel_out[there, :] = panel_out[there, :] - change.astype(jnp.bfloat16).astype(jnp.float32)


def apply_updates(block_rows, place, hi, lo, mine, other, incoming, diag_two, panel_two):
    size = mine.shape[1]
    return pl.pallas_call(
        functools.partial(update_kernel, block_rows),
        out_shape=(
            jax.ShapeDtypeStruct(diag_two.shape, jnp.bfloat16),
            jax.ShapeDtypeStruct(diag_two.shape, jnp.float32),
            jax.ShapeDtypeStruct(panel_two.shape, jnp.float32),
        ),
        in_specs=[SMEM] + [VMEM] * (6 + len(incoming)),
        out_specs=(VMEM,) * 3,
        scratch_shapes=[pltpu.VMEM((size, size), jnp.bfloat16)],
        compiler_params=pltpu.CompilerParams(vmem_limit_bytes=16 * 2**20),
        cost_estimate=pl.CostEstimate(
            flops=5 * size * size * block_rows * len(incoming),
            bytes_accessed=16 * size * size,
            transcendentals=0,
        ),
        name="apply_updates",
    )(place, hi, lo, mine, other, *incoming, diag_two, panel_two)


def exchange(sent):
    received, crossing = [sent[0]], [sent[1]]
    rows = sent[0].shape[0]
    for i, pair in enumerate(sent[2:]):
        pair = shifted(pair, "prow", 2 * i + 2)
        received.append(pair[:rows])
        crossing.append(pair[rows:])
    return received + [shifted(part, "prow", 1) for part in crossing]


def on_device(diag_one, top_rows, panel_one, first_block, target, diag_two, panel_two):
    local = diag_one.shape[0]
    blocks = first_block.shape[0]
    block_rows = panel_one.shape[0] // blocks

    place = jnp.stack([lax.axis_index("pcol"), lax.axis_index("prow")]).astype(jnp.int32)
    half = lax.dynamic_slice_in_dim(
        top_rows, (lax.axis_index("prow") % 2) * (local // 2), local // 2, 0
    )
    turns = [1 << b for b in reversed(range(1, lax.axis_size("pcol").bit_length() - 1))]
    held = [half]
    for s in turns:
        held.append(doubled(held[-1], s))
    own, zeros, sent = route(place, first_block, target, panel_one, held[1])
    if local == NB and lax.axis_size("pcol") == 8:
        got = [cut_piece(diag_one)]
        got += [shifted(got[0], "pcol", s) for s in (2, 4, 6)]
        got[3] = got[3] + zeros
        across = [shifted(part, "pcol", 1) for part in got]
        across[3] = hold(across[3], held[2])
        hi, lo, panel_factor = factor_pieces(place, diag_one.shape[1], got + across, own)
    else:
        whole = lax.all_gather(diag_one, "pcol", axis=0, tiled=True)
        hi, lo, panel_factor = inverse_factor(
            factor_whole_kernel, [VMEM, VMEM], whole.shape[0], (whole, own)
        )
    incoming = exchange(sent)
    top_mine = solve_top(hi, lo, held[-1], shifted(held[-1], "pcol", 1))
    top_other = shifted(top_mine, "prow", 1)
    top_own, diag_next, panel_next = apply_updates(
        block_rows, place, hi, lo, top_mine, top_other, incoming, diag_two, panel_two
    )
    return (panel_factor, top_own, diag_next, panel_next)


def solution(mesh):
    in_specs = (
        P("pcol", None),
        P("pcol", None),
        P(("prow", "pcol"), None),
        P(("prow", "pcol")),
        P(("prow", "pcol")),
        P("pcol", None),
        P(("prow", "pcol"), None),
    )
    out_specs = (
        P(("prow", "pcol"), None),
        P("pcol", None),
        P("pcol", None),
        P(("prow", "pcol"), None),
    )
    return jax.shard_map(
        on_device, mesh=mesh, in_specs=in_specs, out_specs=out_specs, check_vma=False
    )
```

profile of v0, /device:TPU:0, one launch (start us, length us, event | category | flops | bytes accessed | tf_op | source)
XLA Modules:
  0.0 88.8 jit_solution(11372317538144119354)
XLA Ops:
  0.7 1.0 %constant_dynamic-slice_fusion = bf16[64,1024]{1,0:T(8,128)(2,1)S(1)} fusion(bf16[128,1024]{1,0:T(8,128)(2,1)} %param.8, s32[]{:T(128)S(6)} %select_n.17), kind=kLoop, calls=%fused_computation.5 | loop fusion | bytes 262148 | tf_op jit(solution)/shard_map/dynamic_slice | solution.py:442
  1.7 4.1 %collective-permute-start.3 = (bf16[64,1024]{1,0:T(8,128)(2,1)S(1)}, bf16[64,1024]{1,0:T(8,128)(2,1)S(1)}, u32[]{:S(2)}, u32[]{:S(2)}) collective-permute-start(bf16[64,1024]{1,0:T(8,128)(2,1)S(1)} %constant_dynamic-slice_fusion), channel_id=1, source_target_pairs={{0,4},{1,5},{2,6},{3,7},{4,0},{5,1},{6,2},{7,3},{8,12},{9,13},{10,... | collective-permute-start | bytes 393224 | tf_op jit(solution)/shard_map/ppermute | solution.py:241
  5.9 1.6 %collective-permute-start.4 = (f32[64,640]{1,0:T(8,128)S(1)}, f32[64,640]{1,0:T(8,128)S(1)}, u32[]{:S(2)}, u32[]{:S(2)}) collective-permute-start(f32[64,640]{1,0:T(8,128)S(1)} %fusion.refs_0_), channel_id=1, source_target_pairs={{0,1},{1,0},{2,3},{3,2},{4,5},{5,4},{6,7},{7,6},{8,9},{9,8},{10,11... | collective-permute-start | bytes 491528 | tf_op jit(solution)/shard_map/ppermute | solution.py:241
  7.4 1.3 %collective-permute-start.2 = (f32[64,640]{1,0:T(8,128)S(1)}, f32[64,640]{1,0:T(8,128)S(1)}, u32[]{:S(2)}, u32[]{:S(2)}) collective-permute-start(f32[64,640]{1,0:T(8,128)S(1)} %fusion.refs_0_), channel_id=1, source_target_pairs={{0,6},{1,7},{2,4},{3,5},{4,2},{5,3},{6,0},{7,1},{8,14},{9,15},{10,... | collective-permute-start | bytes 491528 | tf_op jit(solution)/shard_map/ppermute | solution.py:241
  8.8 1.7 %collective-permute-start.1 = (f32[64,640]{1,0:T(8,128)S(1)}, f32[64,640]{1,0:T(8,128)S(1)}, u32[]{:S(2)}, u32[]{:S(2)}) collective-permute-start(f32[64,640]{1,0:T(8,128)S(1)} %fusion.refs_0_), channel_id=1, source_target_pairs={{0,4},{1,5},{2,6},{3,7},{4,0},{5,1},{6,2},{7,3},{8,12},{9,13},{10,... | collective-permute-start | bytes 491528 | tf_op jit(solution)/shard_map/ppermute | solution.py:241
  10.5 1.3 %collective-permute-start = (f32[64,640]{1,0:T(8,128)S(1)}, f32[64,640]{1,0:T(8,128)S(1)}, u32[]{:S(2)}, u32[]{:S(2)}) collective-permute-start(f32[64,640]{1,0:T(8,128)S(1)} %fusion.refs_0_), channel_id=1, source_target_pairs={{0,2},{1,3},{2,0},{3,1},{4,6},{5,7},{6,4},{7,5},{8,10},{9,11},{10,... | collective-permute-start | bytes 491528 | tf_op jit(solution)/shard_map/ppermute | solution.py:241
  11.8 8.1 %collective-permute-done.3 = bf16[64,1024]{1,0:T(8,128)(2,1)S(1)} collective-permute-done((bf16[64,1024]{1,0:T(8,128)(2,1)S(1)}, bf16[64,1024]{1,0:T(8,128)(2,1)S(1)}, u32[]{:S(2)}, u32[]{:S(2)}) %collective-permute-start.3) | collective-permute-done | bytes 131104 | tf_op jit(solution)/shard_map/ppermute | solution.py:241
  20.0 0.1 collective-permute-start.8
  20.2 0.7 copy-done.2
  20.8 0.7 copy-done.3
  21.5 0.9 %route_panel.1 = (bf16[512,1024]{1,0:T(8,128)(2,1)S(1)}, f32[64,640]{1,0:T(8,128)S(1)}, bf16[272,1024]{1,0:T(8,128)(2,1)S(1)}, bf16[272,1024]{1,0:T(8,128)(2,1)S(1)}, bf16[544,1024]{1,0:T(8,128)(2,1)S(1)}) custom-call(s32[2]{0:T(128)S(1)} %pad_add_fusion.place_ref, s32[2]{0:T(128)S(1)} %copy-done.2, s32[2]{0:T(128)S(1)} %copy-done.3, ...), custom_call_target="tpu_custom_call" | custom-call | bytes 8388608 | tf_op jit(solution)/shard_map/route_panel/pallas_call | solution.py:335
  22.4 1.9 %collective-permute-start.7 = (f32[64,640]{1,0:T(8,128)S(1)}, f32[64,640]{1,0:T(8,128)S(1)}, u32[]{:S(2)}, u32[]{:S(2)}) collective-permute-start(f32[64,640]{1,0:T(8,128)S(1)} %add.18.refs_3_), channel_id=1, source_target_pairs={{0,1},{1,0},{2,3},{3,2},{4,5},{5,4},{6,7},{7,6},{8,9},{9,8},{10,11... | collective-permute-start | bytes 491528 | tf_op jit(solution)/shard_map/ppermute | solution.py:241
  24.3 1.9 %collective-permute-done.1.refs_2_ = f32[64,640]{1,0:T(8,128)S(1)} collective-permute-done((f32[64,640]{1,0:T(8,128)S(1)}, f32[64,640]{1,0:T(8,128)S(1)}, u32[]{:S(2)}, u32[]{:S(2)}) %collective-permute-start.1) | collective-permute-done | bytes 163872 | tf_op jit(solution)/shard_map/ppermute | solution.py:241
  26.3 1.6 %collective-permute-start.6 = (f32[64,640]{1,0:T(8,128)S(1)}, f32[64,640]{1,0:T(8,128)S(1)}, u32[]{:S(2)}, u32[]{:S(2)}) collective-permute-start(f32[64,640]{1,0:T(8,128)S(1)} %collective-permute-done.1.refs_2_), channel_id=1, source_target_pairs={{0,1},{1,0},{2,3},{3,2},{4,5},{5,4},{6,7},{7,6},{8,9},{9,8},{10,11... | collective-permute-start | bytes 491528 | tf_op jit(solution)/shard_map/ppermute | solution.py:241
  27.8 0.4 collective-permute-done.7.x_ref
  28.2 1.5 %collective-permute-start.5 = (f32[64,640]{1,0:T(8,128)S(1)}, f32[64,640]{1,0:T(8,128)S(1)}, u32[]{:S(2)}, u32[]{:S(2)}) collective-permute-start(f32[64,640]{1,0:T(8,128)S(1)} %collective-permute-done.refs_1_), channel_id=1, source_target_pairs={{0,1},{1,0},{2,3},{3,2},{4,5},{5,4},{6,7},{7,6},{8,9},{9,8},{10,11... | collective-permute-start | bytes 491528 | tf_op jit(solution)/shard_map/ppermute | solution.py:241
  29.7 0.3 collective-permute-done.8
  30.1 0.6 collective-permute-start.10
  30.6 0.1 collective-permute-start.12
  30.7 2.5 %collective-permute-done.6.refs_6_ = f32[64,640]{1,0:T(8,128)S(1)} collective-permute-done((f32[64,640]{1,0:T(8,128)S(1)}, f32[64,640]{1,0:T(8,128)S(1)}, u32[]{:S(2)}, u32[]{:S(2)}) %collective-permute-start.6) | collective-permute-done | bytes 163872 | tf_op jit(solution)/shard_map/ppermute | solution.py:241
  33.3 3.1 %collective-permute-done.5.refs_5_ = f32[64,640]{1,0:T(8,128)S(1)} collective-permute-done((f32[64,640]{1,0:T(8,128)S(1)}, f32[64,640]{1,0:T(8,128)S(1)}, u32[]{:S(2)}, u32[]{:S(2)}) %collective-permute-start.5) | collective-permute-done | bytes 163872 | tf_op jit(solution)/shard_map/ppermute | solution.py:241
  36.4 0.5 collective-permute-start.16
  36.9 1.6 %collective-permute-start.19 = (bf16[544,1024]{1,0:T(8,128)(2,1)S(1)}, bf16[544,1024]{1,0:T(8,128)(2,1)S(1)}, u32[]{:S(2)}, u32[]{:S(2)}) collective-permute-start(bf16[544,1024]{1,0:T(8,128)(2,1)S(1)} %get-tuple-element.21), channel_id=1, source_target_pairs={{0,16},{8,24},{16,0},{24,8},{1,17},{9,25},{17,1},{25,9},{2,18},{10... | collective-permute-start | bytes 3342344 | tf_op jit(solution)/shard_map/ppermute | solution.py:241
  38.5 1.5 %collective-permute-start.17 = (bf16[256,1024]{1,0:T(8,128)(2,1)S(1)}, bf16[256,1024]{1,0:T(8,128)(2,1)S(1)}, u32[]{:S(2)}, u32[]{:S(2)}) collective-permute-start(bf16[256,1024]{1,0:T(8,128)(2,1)S(1)} %pad_maximum_fusion._.first_ref), channel_id=1, source_target_pairs={{0,1},{1,0},{2,3},{3,2},{4,5},{5,4},{6,7},{7,6},{8,9},{9,8},{10,11... | collective-permute-start | bytes 1572872 | tf_op jit(solution)/shard_map/ppermute | solution.py:241
  40.0 34.2 %inverse_factor.1 = (bf16[1024,1024]{1,0:T(8,128)(2,1)S(1)}, bf16[1024,1024]{1,0:T(8,128)(2,1)S(1)}, bf16[512,1024]{1,0:T(8,128)(2,1)}) custom-call(s32[2]{0:T(128)S(1)} %pad_add_fusion.place_ref, f32[64,640]{1,0:T(8,128)S(1)} %fusion.refs_0_, f32[64,640]{1,0:T(8,128)S(1)} %collective-permute-done.refs_1_, f32[64,640]{1,0:T(8,128)S(1)} %collective-permute-done.1.refs_2_, ...), custom_call_target="tpu_custom_call" | custom-call | flops 42949672960 | bytes 8388608 | tf_op jit(solution)/shard_map/inverse_factor/pallas_call | solution.py:220
  74.2 1.8 %solve_top.1.mine_ref = bf16[512,1024]{1,0:T(8,128)(2,1)S(1)} custom-call(bf16[1024,1024]{1,0:T(8,128)(2,1)S(1)} %get-tuple-element.18.hi_ref, bf16[1024,1024]{1,0:T(8,128)(2,1)S(1)} %get-tuple-element.19.lo_ref, bf16[256,1024]{1,0:T(8,128)(2,1)S(1)} %pad_maximum_fusion._.first_ref, bf16[256,1024]{1,0:T(8,128)(2,1)S(1)} %collective-permute-done.17.second_ref), custom_call_target="tpu_custom_call" | custom-call | flops 1610612736 | bytes 8388608 | tf_op jit(solution)/shard_map/solve_top/pallas_call | solution.py:284
  76.2 0.5 collective-permute-start.20
  76.7 0.1 fusion.1
  76.8 0.1 collective-permute-start.21
  76.9 2.7 %collective-permute-done.20.refs_2_ = bf16[272,1024]{1,0:T(8,128)(2,1)S(1)} collective-permute-done((bf16[272,1024]{1,0:T(8,128)(2,1)S(1)}, bf16[272,1024]{1,0:T(8,128)(2,1)S(1)}, u32[]{:S(2)}, u32[]{:S(2)}) %collective-permute-start.20) | collective-permute-done | bytes 557088 | tf_op jit(solution)/shard_map/ppermute | solution.py:241
  79.6 0.8 collective-permute-done.21.refs_3_
  80.4 8.3 %apply_updates.1 = (bf16[128,1024]{1,0:T(8,128)(2,1)}, f32[128,1024]{1,0:T(8,128)}, f32[512,1024]{1,0:T(8,128)}) custom-call(s32[2]{0:T(128)S(1)} %pad_add_fusion.place_ref, bf16[1024,1024]{1,0:T(8,128)(2,1)S(1)} %get-tuple-element.18.hi_ref, bf16[1024,1024]{1,0:T(8,128)(2,1)S(1)} %get-tuple-element.19.lo_ref, bf16[512,1024]{1,0:T(8,128)(2,1)S(1)} %solve_top.1.mine_ref, ...), custom_call_target="tpu_custom_call" | custom-call | flops 5368709120 | bytes 16777216 | tf_op jit(solution)/shard_map/apply_updates/pallas_call | solution.py:406
  (37 shorter events, 0.4 us)
Async XLA Ops:
  0.6 5.2 %copy-start = (f32[128,1024]{1,0:T(8,128)S(1)}, f32[128,1024]{1,0:T(8,128)}, u32[]{:S(2)}) copy-start(f32[128,1024]{1,0:T(8,128)} %param.7) | copy-start | bytes 1572868
  0.6 19.5 %copy-start.1 = (bf16[512,1024]{1,0:T(8,128)(2,1)S(1)}, bf16[512,1024]{1,0:T(8,128)(2,1)}, u32[]{:S(2)}) copy-start(bf16[512,1024]{1,0:T(8,128)(2,1)} %panel_ref.1) | copy-start | bytes 3145732
  1.7 18.3 %collective-permute-start.3 = (bf16[64,1024]{1,0:T(8,128)(2,1)S(1)}, bf16[64,1024]{1,0:T(8,128)(2,1)S(1)}, u32[]{:S(2)}, u32[]{:S(2)}) collective-permute-start(bf16[64,1024]{1,0:T(8,128)(2,1)S(1)} %constant_dynamic-slice_fusion), channel_id=1, source_target_pairs={{0,4},{1,5},{2,6},{3,7},{4,0},{5,1},{6,2},{7,3},{8,12},{9,13},{10,... | collective-permute-start | bytes 393224 | tf_op jit(solution)/shard_map/ppermute | solution.py:241
  5.9 18.4 %collective-permute-start.4 = (f32[64,640]{1,0:T(8,128)S(1)}, f32[64,640]{1,0:T(8,128)S(1)}, u32[]{:S(2)}, u32[]{:S(2)}) collective-permute-start(f32[64,640]{1,0:T(8,128)S(1)} %fusion.refs_0_), channel_id=1, source_target_pairs={{0,1},{1,0},{2,3},{3,2},{4,5},{5,4},{6,7},{7,6},{8,9},{9,8},{10,11... | collective-permute-start | bytes 491528 | tf_op jit(solution)/shard_map/ppermute | solution.py:241
  7.4 14.9 %collective-permute-start.2 = (f32[64,640]{1,0:T(8,128)S(1)}, f32[64,640]{1,0:T(8,128)S(1)}, u32[]{:S(2)}, u32[]{:S(2)}) collective-permute-start(f32[64,640]{1,0:T(8,128)S(1)} %fusion.refs_0_), channel_id=1, source_target_pairs={{0,6},{1,7},{2,4},{3,5},{4,2},{5,3},{6,0},{7,1},{8,14},{9,15},{10,... | collective-permute-start | bytes 491528 | tf_op jit(solution)/shard_map/ppermute | solution.py:241
  8.8 17.5 %collective-permute-start.1 = (f32[64,640]{1,0:T(8,128)S(1)}, f32[64,640]{1,0:T(8,128)S(1)}, u32[]{:S(2)}, u32[]{:S(2)}) collective-permute-start(f32[64,640]{1,0:T(8,128)S(1)} %fusion.refs_0_), channel_id=1, source_target_pairs={{0,4},{1,5},{2,6},{3,7},{4,0},{5,1},{6,2},{7,3},{8,12},{9,13},{10,... | collective-permute-start | bytes 491528 | tf_op jit(solution)/shard_map/ppermute | solution.py:241
  10.5 15.8 %collective-permute-start = (f32[64,640]{1,0:T(8,128)S(1)}, f32[64,640]{1,0:T(8,128)S(1)}, u32[]{:S(2)}, u32[]{:S(2)}) collective-permute-start(f32[64,640]{1,0:T(8,128)S(1)} %fusion.refs_0_), channel_id=1, source_target_pairs={{0,2},{1,3},{2,0},{3,1},{4,6},{5,7},{6,4},{7,5},{8,10},{9,11},{10,... | collective-permute-start | bytes 491528 | tf_op jit(solution)/shard_map/ppermute | solution.py:241
  20.0 10.0 %collective-permute-start.8 = (bf16[128,1024]{1,0:T(8,128)(2,1)S(1)}, bf16[128,1024]{1,0:T(8,128)(2,1)S(1)}, u32[]{:S(2)}, u32[]{:S(2)}) collective-permute-start(bf16[128,1024]{1,0:T(8,128)(2,1)S(1)} %pad_maximum_fusion.1._), channel_id=1, source_target_pairs={{0,2},{1,3},{2,0},{3,1},{4,6},{5,7},{6,4},{7,5},{8,10},{9,11},{10,... | collective-permute-start | bytes 786440 | tf_op jit(solution)/shard_map/ppermute | solution.py:241
  20.2 0.7 copy-start.2
  20.8 0.7 copy-start.3
  22.4 5.8 %collective-permute-start.7 = (f32[64,640]{1,0:T(8,128)S(1)}, f32[64,640]{1,0:T(8,128)S(1)}, u32[]{:S(2)}, u32[]{:S(2)}) collective-permute-start(f32[64,640]{1,0:T(8,128)S(1)} %add.18.refs_3_), channel_id=1, source_target_pairs={{0,1},{1,0},{2,3},{3,2},{4,5},{5,4},{6,7},{7,6},{8,9},{9,8},{10,11... | collective-permute-start | bytes 491528 | tf_op jit(solution)/shard_map/ppermute | solution.py:241
  24.3 5.7 %collective-permute-start.9 = (f32[64,640]{1,0:T(8,128)S(1)}, f32[64,640]{1,0:T(8,128)S(1)}, u32[]{:S(2)}, u32[]{:S(2)}) collective-permute-start(f32[64,640]{1,0:T(8,128)S(1)} %fusion.refs_0_), channel_id=1, source_target_pairs={{0,8},{8,0},{16,24},{24,16},{1,9},{9,1},{17,25},{25,17},{2,10},{10... | collective-permute-start | bytes 491528 | tf_op jit(solution)/shard_map/ppermute | solution.py:241
  26.3 4.4 %collective-permute-start.13 = (f32[64,640]{1,0:T(8,128)S(1)}, f32[64,640]{1,0:T(8,128)S(1)}, u32[]{:S(2)}, u32[]{:S(2)}) collective-permute-start(f32[64,640]{1,0:T(8,128)S(1)} %collective-permute-done.4.refs_4_), channel_id=1, source_target_pairs={{0,8},{8,0},{16,24},{24,16},{1,9},{9,1},{17,25},{25,17},{2,10},{10... | collective-permute-start | bytes 491528 | tf_op jit(solution)/shard_map/ppermute | solution.py:241
  26.3 7.0 %collective-permute-start.6 = (f32[64,640]{1,0:T(8,128)S(1)}, f32[64,640]{1,0:T(8,128)S(1)}, u32[]{:S(2)}, u32[]{:S(2)}) collective-permute-start(f32[64,640]{1,0:T(8,128)S(1)} %collective-permute-done.1.refs_2_), channel_id=1, source_target_pairs={{0,1},{1,0},{2,3},{3,2},{4,5},{5,4},{6,7},{7,6},{8,9},{9,8},{10,11... | collective-permute-start | bytes 491528 | tf_op jit(solution)/shard_map/ppermute | solution.py:241
  28.2 8.2 %collective-permute-start.5 = (f32[64,640]{1,0:T(8,128)S(1)}, f32[64,640]{1,0:T(8,128)S(1)}, u32[]{:S(2)}, u32[]{:S(2)}) collective-permute-start(f32[64,640]{1,0:T(8,128)S(1)} %collective-permute-done.refs_1_), channel_id=1, source_target_pairs={{0,1},{1,0},{2,3},{3,2},{4,5},{5,4},{6,7},{7,6},{8,9},{9,8},{10,11... | collective-permute-start | bytes 491528 | tf_op jit(solution)/shard_map/ppermute | solution.py:241
  30.0 6.4 %collective-permute-start.11 = (f32[64,640]{1,0:T(8,128)S(1)}, f32[64,640]{1,0:T(8,128)S(1)}, u32[]{:S(2)}, u32[]{:S(2)}) collective-permute-start(f32[64,640]{1,0:T(8,128)S(1)} %collective-permute-done.1.refs_2_), channel_id=1, source_target_pairs={{0,8},{8,0},{16,24},{24,16},{1,9},{9,1},{17,25},{25,17},{2,10},{10... | collective-permute-start | bytes 491528 | tf_op jit(solution)/shard_map/ppermute | solution.py:241
  30.1 6.9 %collective-permute-start.10 = (f32[64,640]{1,0:T(8,128)S(1)}, f32[64,640]{1,0:T(8,128)S(1)}, u32[]{:S(2)}, u32[]{:S(2)}) collective-permute-start(f32[64,640]{1,0:T(8,128)S(1)} %collective-permute-done.refs_1_), channel_id=1, source_target_pairs={{0,8},{8,0},{16,24},{24,16},{1,9},{9,1},{17,25},{25,17},{2,10},{10... | collective-permute-start | bytes 491528 | tf_op jit(solution)/shard_map/ppermute | solution.py:241
  30.6 7.9 %collective-permute-start.12 = (f32[64,640]{1,0:T(8,128)S(1)}, f32[64,640]{1,0:T(8,128)S(1)}, u32[]{:S(2)}, u32[]{:S(2)}) collective-permute-start(f32[64,640]{1,0:T(8,128)S(1)} %add.18.refs_3_), channel_id=1, source_target_pairs={{0,8},{8,0},{16,24},{24,16},{1,9},{9,1},{17,25},{25,17},{2,10},{10... | collective-permute-start | bytes 491528 | tf_op jit(solution)/shard_map/ppermute | solution.py:241
  33.3 6.7 %collective-permute-start.15 = (f32[64,640]{1,0:T(8,128)S(1)}, f32[64,640]{1,0:T(8,128)S(1)}, u32[]{:S(2)}, u32[]{:S(2)}) collective-permute-start(f32[64,640]{1,0:T(8,128)S(1)} %collective-permute-done.6.refs_6_), channel_id=1, source_target_pairs={{0,8},{8,0},{16,24},{24,16},{1,9},{9,1},{17,25},{25,17},{2,10},{10... | collective-permute-start | bytes 491528 | tf_op jit(solution)/shard_map/ppermute | solution.py:241
  36.4 3.6 %collective-permute-start.14 = (f32[64,640]{1,0:T(8,128)S(1)}, f32[64,640]{1,0:T(8,128)S(1)}, u32[]{:S(2)}, u32[]{:S(2)}) collective-permute-start(f32[64,640]{1,0:T(8,128)S(1)} %collective-permute-done.5.refs_5_), channel_id=1, source_target_pairs={{0,8},{8,0},{16,24},{24,16},{1,9},{9,1},{17,25},{25,17},{2,10},{10... | collective-permute-start | bytes 491528 | tf_op jit(solution)/shard_map/ppermute | solution.py:241
  36.4 3.6 %collective-permute-start.16 = (f32[64,640]{1,0:T(8,128)S(1)}, f32[64,640]{1,0:T(8,128)S(1)}, u32[]{:S(2)}, u32[]{:S(2)}) collective-permute-start(f32[64,640]{1,0:T(8,128)S(1)} %hold_piece.1.refs_7_), channel_id=1, source_target_pairs={{0,8},{8,0},{16,24},{24,16},{1,9},{9,1},{17,25},{25,17},{2,10},{10... | collective-permute-start | bytes 491528 | tf_op jit(solution)/shard_map/ppermute | solution.py:241
  36.9 39.8 %collective-permute-start.19 = (bf16[544,1024]{1,0:T(8,128)(2,1)S(1)}, bf16[544,1024]{1,0:T(8,128)(2,1)S(1)}, u32[]{:S(2)}, u32[]{:S(2)}) collective-permute-start(bf16[544,1024]{1,0:T(8,128)(2,1)S(1)} %get-tuple-element.21), channel_id=1, source_target_pairs={{0,16},{8,24},{16,0},{24,8},{1,17},{9,25},{17,1},{25,9},{2,18},{10... | collective-permute-start | bytes 3342344 | tf_op jit(solution)/shard_map/ppermute | solution.py:241
  38.5 35.7 %collective-permute-start.17 = (bf16[256,1024]{1,0:T(8,128)(2,1)S(1)}, bf16[256,1024]{1,0:T(8,128)(2,1)S(1)}, u32[]{:S(2)}, u32[]{:S(2)}) collective-permute-start(bf16[256,1024]{1,0:T(8,128)(2,1)S(1)} %pad_maximum_fusion._.first_ref), channel_id=1, source_target_pairs={{0,1},{1,0},{2,3},{3,2},{4,5},{5,4},{6,7},{7,6},{8,9},{9,8},{10,11... | collective-permute-start | bytes 1572872 | tf_op jit(solution)/shard_map/ppermute | solution.py:241
  76.1 4.3 %copy-start.4 = (bf16[512,1024]{1,0:T(8,128)(2,1)S(1)}, bf16[512,1024]{1,0:T(8,128)(2,1)}, u32[]{:S(2)}) copy-start(bf16[512,1024]{1,0:T(8,128)(2,1)} %refs_5_.1) | copy-start | bytes 3145732
  76.1 4.3 %copy-start.5 = (f32[128,1024]{1,0:T(8,128)S(1)}, f32[128,1024]{1,0:T(8,128)}, u32[]{:S(2)}) copy-start(f32[128,1024]{1,0:T(8,128)} %refs_4_.1) | copy-start | bytes 1572868
  76.1 4.3 %collective-permute-start.18 = (bf16[512,1024]{1,0:T(8,128)(2,1)S(1)}, bf16[512,1024]{1,0:T(8,128)(2,1)S(1)}, u32[]{:S(2)}, u32[]{:S(2)}) collective-permute-start(bf16[512,1024]{1,0:T(8,128)(2,1)S(1)} %solve_top.1.mine_ref), channel_id=1, source_target_pairs={{0,8},{8,0},{16,24},{24,16},{1,9},{9,1},{17,25},{25,17},{2,10},{10... | collective-permute-start | bytes 3145736 | tf_op jit(solution)/shard_map/ppermute | solution.py:241
  76.2 3.4 %collective-permute-start.20 = (bf16[272,1024]{1,0:T(8,128)(2,1)S(1)}, bf16[272,1024]{1,0:T(8,128)(2,1)S(1)}, u32[]{:S(2)}, u32[]{:S(2)}) collective-permute-start(bf16[272,1024]{1,0:T(8,128)(2,1)S(1)} %get-tuple-element.22), channel_id=1, source_target_pairs={{0,8},{8,0},{16,24},{24,16},{1,9},{9,1},{17,25},{25,17},{2,10},{10... | collective-permute-start | bytes 1671176 | tf_op jit(solution)/shard_map/ppermute | solution.py:241
  76.8 3.7 %collective-permute-start.21 = (bf16[272,1024]{1,0:T(8,128)(2,1)S(1)}, bf16[272,1024]{1,0:T(8,128)(2,1)S(1)}, u32[]{:S(2)}, u32[]{:S(2)}) collective-permute-start(bf16[272,1024]{1,0:T(8,128)(2,1)S(1)} %get-tuple-element.26), channel_id=1, source_target_pairs={{0,8},{8,0},{16,24},{24,16},{1,9},{9,1},{17,25},{25,17},{2,10},{10... | collective-permute-start | bytes 1671176 | tf_op jit(solution)/shard_map/ppermute | solution.py:241
where the time goes:
time: 88.9 us; the launch traced here: 88.8 us
  Pallas kernels  45.3 us (51%)
  starting transfers between devices  20.1 us (23%)
  waiting for transfers between devices  20 us (22%)
  local copies, waits for them, and re-layouts  2.46 us (3%)
    pallas_call x1, Pallas kernels, inverse_factor(): pl.pallas_call(kernel, out_shape=(half, half, jax.ShapeDtypeStruct(operan...  34.2 us
    ppermute x22, starting transfers between devices, shifted(): lax.ppermute(x, axis, [(i, i ^ s) for i in range(lax.axis_size(axis))])  20.1 us
    ppermute x22, waiting for transfers between devices, shifted(): lax.ppermute(x, axis, [(i, i ^ s) for i in range(lax.axis_size(axis))])  20 us
    pallas_call x1, Pallas kernels, apply_updates(): pl.pallas_call(functools.partial(update_kernel, block_rows), out_shape=(j...  8.35 us
    pallas_call x1, Pallas kernels, solve_top(): pl.pallas_call(top_kernel, out_shape=jax.ShapeDtypeStruct((rows, size), j...  1.84 us
  transfers between devices with their start and end apart: 22, of which 8 were waited for; matrix products, arithmetic and copies ran while one was open for 0% of the time, Pallas kernels for 42%

commit v1 on v0

--- a/solution.py
+++ b/solution.py
@@ -14,22 +14,24 @@
 SMEM = pl.BlockSpec(memory_space=pltpu.SMEM)
 
 
-def split3(x):
+def split2(x):
     hi = x.astype(jnp.bfloat16)
-    rest = x - hi.astype(jnp.float32)
-    mid = rest.astype(jnp.bfloat16)
-    low = (rest - mid.astype(jnp.float32)).astype(jnp.bfloat16)
-    return hi, mid, low
+    return hi, (x - hi.astype(jnp.float32)).astype(jnp.bfloat16)
 
 
 def left_terms(x):
-    hi, mid, low = split3(x)
-    return jnp.concatenate([hi, hi, mid], 0)
+    hi, mid = split2(x)
+    return jnp.concatenate([mid, hi, hi], 0)
 
 
 def right_terms(x):
-    hi, mid, low = split3(x)
+    hi, mid = split2(x)
     return jnp.concatenate([hi, mid, hi], 0)
+
+
+def both_terms(x):
+    hi, mid = split2(x)
+    return jnp.concatenate([hi, mid, hi, hi], 0)
 
 
 def dot_tn(left, right):
@@ -142,17 +144,17 @@
 
 def factor_pieces_kernel(pieces, place_ref, *refs):
     *rest, sems = refs[pieces:]
-    assemble_pieces(place_ref, refs[:pieces], rest[4], sems)
+    assemble_pieces(place_ref, refs[:pieces], rest[2], sems)
     factor_kernel(*rest)
 
 
 def factor_whole_kernel(diag_ref, *refs):
     *rest, _ = refs
-    rest[4][...] = diag_ref[...]
+    rest[2][...] = diag_ref[...]
     factor_kernel(*rest)
 
 
-def factor_kernel(own_ref, hi_ref, lo_ref, own_out, work, block, left, right):
+def factor_kernel(hi_ref, lo_ref, work, block, terms):
     size = work.shape[0]
     count = size // NB
     same = lax.broadcasted_iota(jnp.int32, (NB, NB), 0) == lax.broadcasted_iota(
@@ -166,12 +168,11 @@
     def solve(k, inverse, columns):
         solved = dot_tn(inverse, right_terms(work[strip(k), columns]))
         work[strip(k), columns] = solved
-        left[k % 2, :, columns] = left_terms(solved)
-        right[k % 2, :, columns] = right_terms(solved)
+        terms[k % 2, :, columns] = both_terms(solved)
 
     def update(i, k, columns):
         work[strip(i), columns] = work[strip(i), columns] - dot_tn(
-            left[k % 2, :, strip(i)], right[k % 2, :, columns]
+            terms[k % 2, NB:, strip(i)], terms[k % 2, : 3 * NB, columns]
         )
 
     def rest(k, inverse, plain):
@@ -180,7 +181,7 @@
         if k:
             solve(k, inverse, strip(0, k))
         work[strip(k), strip(k)] = plain
-        right[k % 2, :, strip(k)] = right_terms(plain)
+        terms[k % 2, :, strip(k)] = both_terms(plain)
         upto = (k + 1) * NB
         value = work[strip(k), :upto]
         hi = value.astype(jnp.bfloat16)
@@ -190,8 +191,6 @@
         if upto < size:
             hi_ref[strip(k), upto:] = jnp.zeros((NB, size - upto), jnp.bfloat16)
             lo_ref[strip(k), upto:] = jnp.zeros((NB, size - upto), jnp.bfloat16)
-        rows = own_ref[:, :upto]
-        own_out[:, strip(k)] = (dot_nt(rows, hi) + dot_nt(rows, lo)).astype(jnp.bfloat16)
         for i in range(k + 1, count):
             first = i + 1 if i == k + 1 else i
             if first < count:
@@ -219,14 +218,13 @@
     half = jax.ShapeDtypeStruct((size, size), jnp.bfloat16)
     return pl.pallas_call(
         kernel,
-        out_shape=(half, half, jax.ShapeDtypeStruct(operands[-1].shape, jnp.bfloat16)),
+        out_shape=(half, half),
         in_specs=in_specs,
-        out_specs=(VMEM,) * 3,
+        out_specs=(VMEM,) * 2,
         scratch_shapes=[
             pltpu.VMEM((size, size), jnp.float32),
             pltpu.VMEM((2, NB, 2 * NB), jnp.float32),
-            pltpu.VMEM((2, 3 * NB, size), jnp.bfloat16),
-            pltpu.VMEM((2, 3 * NB, size), jnp.bfloat16),
+            pltpu.VMEM((2, 4 * NB, size), jnp.bfloat16),
             pltpu.SemaphoreType.DMA((80,)),
         ],
         compiler_params=pltpu.CompilerParams(vmem_limit_bytes=20 * 2**20),
@@ -250,48 +248,43 @@
     )
 
 
-def factor_pieces(place, size, mine, own):
+def factor_pieces(place, size, mine):
     pieces = mine + [shifted(part, "prow", 1) for part in mine]
     return inverse_factor(
         functools.partial(factor_pieces_kernel, len(pieces)),
-        [SMEM] + [ANY] * len(pieces) + [VMEM],
+        [SMEM] + [ANY] * len(pieces),
         size,
-        (place, *pieces, own),
-    )
-
-
-def solve_rows(x, hi_ref, lo_ref):
+        (place, *pieces),
+    )
+
+
+def solve_rows(x, hi_ref, lo_ref, out_ref):
     size = hi_ref.shape[0]
     width = 256
-    parts = []
     for j in range(size // width):
         rows, upto = slice(j * width, (j + 1) * width), (j + 1) * width
-        parts.append(
+        out_ref[:, rows] = (
             dot_nt(x[:, :upto], hi_ref[rows, :upto]) + dot_nt(x[:, :upto], lo_ref[rows, :upto])
-        )
-    return jnp.concatenate(parts, 1).astype(jnp.bfloat16)
-
-
-def top_kernel(hi_ref, lo_ref, first_ref, second_ref, out_ref):
-    rows = first_ref.shape[0]
-    for c, ref in enumerate((first_ref, second_ref)):
-        out_ref[c * rows : (c + 1) * rows, :] = solve_rows(ref[...], hi_ref, lo_ref)
-
-
-def solve_top(hi, lo, first, second):
+        ).astype(jnp.bfloat16)
+
+
+def solve_kernel(hi_ref, lo_ref, x_ref, out_ref):
+    solve_rows(x_ref, hi_ref, lo_ref, out_ref)
+
+
+def solve(hi, lo, x, name):
     size = hi.shape[0]
-    rows = 2 * first.shape[0]
     return pl.pallas_call(
-        top_kernel,
-        out_shape=jax.ShapeDtypeStruct((rows, size), jnp.bfloat16),
-        in_specs=[VMEM] * 4,
+        solve_kernel,
+        out_shape=jax.ShapeDtypeStruct(x.shape, jnp.bfloat16),
+        in_specs=[VMEM] * 3,
         out_specs=VMEM,
         compiler_params=pltpu.CompilerParams(vmem_limit_bytes=12 * 2**20),
         cost_estimate=pl.CostEstimate(
-            flops=3 * size * size * rows, bytes_accessed=8 * size * size, transcendentals=0
-        ),
-        name="solve_top",
-    )(hi, lo, first, second)
+            flops=3 * size * x.size, bytes_accessed=8 * size * size, transcendentals=0
+        ),
+        name=name,
+    )(hi, lo, x)
 
 
 def route_kernel(
@@ -341,7 +334,7 @@
         + tuple(
             jax.ShapeDtypeStruct((n * (block_rows + 16), size), jnp.bfloat16) for n in sent
         ),
-        in_specs=[SMEM] * 3 + [VMEM, ANY],
+        in_specs=[SMEM] * 3 + [VMEM] * 2,
         out_specs=(VMEM,) * (2 + len(sent)),
         compiler_params=pltpu.CompilerParams(vmem_limit_bytes=12 * 2**20),
         cost_estimate=pl.CostEstimate(
@@ -360,7 +353,7 @@
     return pl.pallas_call(
         hold_kernel,
         out_shape=jax.ShapeDtypeStruct(x.shape, x.dtype),
-        in_specs=[VMEM, ANY],
+        in_specs=[VMEM, VMEM],
         out_specs=VMEM,
         compiler_params=pltpu.CompilerParams(vmem_limit_bytes=4 * 2**20),
         cost_estimate=pl.CostEstimate(
@@ -375,30 +368,36 @@
 
 
 def update_kernel(block_rows, place_ref, hi_ref, lo_ref, mine_ref, other_ref, *refs):
-    incoming = refs[:-6]
-    diag_ref, panel_ref, top_out, diag_out, panel_out, top_all = refs[-6:]
+    incoming = refs[:-8]
+    diag_ref, panel_ref, top_out, diag_out, panel_out, top_all, received, solved = refs[-8:]
+    for i, ref in enumerate(incoming):
+        received[i * block_rows : (i + 1) * block_rows, :] = ref[:block_rows, :]
+    solve_rows(received, hi_ref, lo_ref, solved)
     local = top_out.shape[0]
     half = local // 2
     strips = mine_ref.shape[0] // half
-    bits = strips.bit_length() - 1
     column, core = place_ref[0], place_ref[1] % 2
     for c, ref in enumerate((mine_ref, other_ref)):
         for slot in range(strips):
-            strip = column ^ sum(((slot >> b) & 1) << (bits - 1 - b) for b in range(bits))
-            row = pl.multiple_of(strip * local + (core ^ c) * half, half)
+            row = pl.multiple_of((column ^ slot) * local + (core ^ c) * half, half)
             top_all[pl.ds(row, half), :] = ref[slot * half : (slot + 1) * half, :]
     mine = top_all[pl.ds(pl.multiple_of(column * local, local), local), :]
     top_out[...] = mine
     diag_out[...] = diag_ref[...] - dot_nt(mine, top_all[...])
     panel_out[...] = panel_ref[...].astype(jnp.float32)
-    for ref in incoming:
-        solved = solve_rows(ref[:block_rows, :], hi_ref, lo_ref)
-        change = dot_nt(solved, top_all[...])
-        slot = jnp.max(ref[block_rows : block_rows + 16, :NB].astype(jnp.float32))
-        there = pl.ds(
-            pl.multiple_of(slot.astype(jnp.int32) * block_rows, block_rows), block_rows
-        )
-        panel_out[there, :] = panel_out[there, :] - change.astype(jnp.bfloat16).astype(jnp.float32)
+    slots = [
+        jnp.max(ref[block_rows : block_rows + 16, :NB].astype(jnp.float32)).astype(jnp.int32)
+        for ref in incoming
+    ]
+    width = 256
+    for j in range(0, top_all.shape[0], width):
+        columns = slice(j, j + width)
+        change = dot_nt(solved[...], top_all[columns, :]).astype(jnp.bfloat16).astype(jnp.float32)
+        for i, slot in enumerate(slots):
+            there = pl.ds(pl.multiple_of(slot * block_rows, block_rows), block_rows)
+            panel_out[there, columns] = (
+                panel_out[there, columns] - change[i * block_rows : (i + 1) * block_rows]
+            )
 
 
 def apply_updates(block_rows, place, hi, lo, mine, other, incoming, diag_two, panel_two):
@@ -412,8 +411,12 @@
         ),
         in_specs=[SMEM] + [VMEM] * (6 + len(incoming)),
         out_specs=(VMEM,) * 3,
-        scratch_shapes=[pltpu.VMEM((size, size), jnp.bfloat16)],
-        compiler_params=pltpu.CompilerParams(vmem_limit_bytes=16 * 2**20),
+        scratch_shapes=[
+            pltpu.VMEM((size, size), jnp.bfloat16),
+            pltpu.VMEM((block_rows * len(incoming), size), jnp.bfloat16),
+            pltpu.VMEM((block_rows * len(incoming), size), jnp.bfloat16),
+        ],
+        compiler_params=pltpu.CompilerParams(vmem_limit_bytes=24 * 2**20),
         cost_estimate=pl.CostEstimate(
             flops=5 * size * size * block_rows * len(incoming),
             bytes_accessed=16 * size * size,
@@ -442,26 +445,24 @@
     half = lax.dynamic_slice_in_dim(
         top_rows, (lax.axis_index("prow") % 2) * (local // 2), local // 2, 0
     )
-    turns = [1 << b for b in reversed(range(1, lax.axis_size("pcol").bit_length() - 1))]
     held = [half]
-    for s in turns:
-        held.append(doubled(held[-1], s))
+    while 2 * len(held[-1]) < len(half) * lax.axis_size("pcol"):
+        held.append(doubled(held[-1], len(held[-1]) // len(half)))
     own, zeros, sent = route(place, first_block, target, panel_one, held[1])
     if local == NB and lax.axis_size("pcol") == 8:
         got = [cut_piece(diag_one)]
-        got += [shifted(got[0], "pcol", s) for s in (2, 4, 6)]
-        got[3] = got[3] + zeros
+        got += [shifted(got[0], "pcol", s) for s in (2, 4)]
+        got.append(shifted(got[2], "pcol", 2) + zeros)
         across = [shifted(part, "pcol", 1) for part in got]
         across[3] = hold(across[3], held[2])
-        hi, lo, panel_factor = factor_pieces(place, diag_one.shape[1], got + across, own)
+        hi, lo = factor_pieces(place, diag_one.shape[1], got + across)
     else:
         whole = lax.all_gather(diag_one, "pcol", axis=0, tiled=True)
-        hi, lo, panel_factor = inverse_factor(
-            factor_whole_kernel, [VMEM, VMEM], whole.shape[0], (whole, own)
-        )
+        hi, lo = inverse_factor(factor_whole_kernel, [VMEM], whole.shape[0], (whole,))
     incoming = exchange(sent)
-    top_mine = solve_top(hi, lo, held[-1], shifted(held[-1], "pcol", 1))
+    top_mine = solve(hi, lo, doubled(held[-1], lax.axis_size("pcol") // 2), "solve_top")
     top_other = shifted(top_mine, "prow", 1)
+    panel_factor = solve(hi, lo, own, "solve_own")
     top_own, diag_next, panel_next = apply_updates(
         block_rows, place, hi, lo, top_mine, top_other, incoming, diag_two, panel_two
     )

time: 88.9 us -> 82.3 us (0.926)
  waiting for transfers between devices: 20 us -> 14.5 us
  Pallas kernels: 45.3 us -> 43.9 us
    ppermute x22, waiting for transfers between devices: 20 us -> 14.5 us  [shifted(): lax.ppermute(x, axis, [(i, i ^ s) for i in range(lax.axis_size(axis))])]
    pallas_call x2 -> x3, Pallas kernels: 36 us -> 34.7 us  [the longest x1 30.6 us: inverse_factor(): pl.pallas_call(kernel, out_shape=(half, half), in_specs=in_specs, out_spe...]
    unnamed x12, local copies, waits for them, and re-layouts: 1.34 us -> 2.33 us
  transfers between devices with their start and end apart: 22 -> 22, of which waited for: 8 -> 7; matrix products, arithmetic and copies ran while one was open for 0% -> 1% of each run, Pallas kernels for 42% -> 43%
where the time goes in v1:
time: 82.3 us; the launch traced here: 82.1 us
  Pallas kernels  43.9 us (53%)
  starting transfers between devices  19.4 us (24%)
  waiting for transfers between devices  14.5 us (18%)
  local copies, waits for them, and re-layouts  3.34 us (4%)
    pallas_call x1, Pallas kernels, inverse_factor(): pl.pallas_call(kernel, out_shape=(half, half), in_specs=in_specs, out_spe...  30.6 us
    ppermute x22, starting transfers between devices, shifted(): lax.ppermute(x, axis, [(i, i ^ s) for i in range(lax.axis_size(axis))])  19.4 us
    ppermute x22, waiting for transfers between devices, shifted(): lax.ppermute(x, axis, [(i, i ^ s) for i in range(lax.axis_size(axis))])  14.5 us
    pallas_call x1, Pallas kernels, apply_updates(): pl.pallas_call(functools.partial(update_kernel, block_rows), out_shape=(j...  8.22 us
    pallas_call x2, Pallas kernels, solve(): pl.pallas_call(solve_kernel, out_shape=jax.ShapeDtypeStruct(x.shape, jnp....  4.11 us
    unnamed x12, local copies, waits for them, and re-layouts  2.33 us
  transfers between devices with their start and end apart: 22, of which 7 were waited for; matrix products, arithmetic and copies ran while one was open for 1% of the time, Pallas kernels for 43%

profile of v1, /device:TPU:0, one launch (start us, length us, event | category | flops | bytes accessed | tf_op | source)
XLA Modules:
  0.0 82.1 jit_solution(5693573879962045468)
XLA Ops:
  0.7 1.0 %copy-done = f32[128,1024]{1,0:T(8,128)S(1)} copy-done((f32[128,1024]{1,0:T(8,128)S(1)}, f32[128,1024]{1,0:T(8,128)}, u32[]{:S(2)}) %copy-start) | copy-done | bytes 524312
  1.8 4.1 %collective-permute-start.1 = (f32[64,640]{1,0:T(8,128)S(1)}, f32[64,640]{1,0:T(8,128)S(1)}, u32[]{:S(2)}, u32[]{:S(2)}) collective-permute-start(f32[64,640]{1,0:T(8,128)S(1)} %fusion.refs_0_), channel_id=1, source_target_pairs={{0,4},{1,5},{2,6},{3,7},{4,0},{5,1},{6,2},{7,3},{8,12},{9,13},{10,... | collective-permute-start | bytes 491528 | tf_op jit(solution)/shard_map/ppermute | solution.py:239
  5.9 0.9 %constant_dynamic-slice_fusion = bf16[64,1024]{1,0:T(8,128)(2,1)S(1)} fusion(bf16[128,1024]{1,0:T(8,128)(2,1)} %param.8, s32[]{:T(128)S(6)} %select_n.17), kind=kLoop, calls=%fused_computation.6 | loop fusion | bytes 262148 | tf_op jit(solution)/shard_map/dynamic_slice | solution.py:445
  6.8 1.6 %collective-permute-start.3 = (bf16[64,1024]{1,0:T(8,128)(2,1)S(1)}, bf16[64,1024]{1,0:T(8,128)(2,1)S(1)}, u32[]{:S(2)}, u32[]{:S(2)}) collective-permute-start(bf16[64,1024]{1,0:T(8,128)(2,1)S(1)} %constant_dynamic-slice_fusion), channel_id=1, source_target_pairs={{0,1},{1,0},{2,3},{3,2},{4,5},{5,4},{6,7},{7,6},{8,9},{9,8},{10,11... | collective-permute-start | bytes 393224 | tf_op jit(solution)/shard_map/ppermute | solution.py:239
  8.3 0.5 collective-permute-start.4
  8.9 1.6 %collective-permute-start = (f32[64,640]{1,0:T(8,128)S(1)}, f32[64,640]{1,0:T(8,128)S(1)}, u32[]{:S(2)}, u32[]{:S(2)}) collective-permute-start(f32[64,640]{1,0:T(8,128)S(1)} %fusion.refs_0_), channel_id=1, source_target_pairs={{0,2},{1,3},{2,0},{3,1},{4,6},{5,7},{6,4},{7,5},{8,10},{9,11},{10,... | collective-permute-start | bytes 491528 | tf_op jit(solution)/shard_map/ppermute | solution.py:239
  10.4 3.2 %collective-permute-done.1.refs_2_ = f32[64,640]{1,0:T(8,128)S(1)} collective-permute-done((f32[64,640]{1,0:T(8,128)S(1)}, f32[64,640]{1,0:T(8,128)S(1)}, u32[]{:S(2)}, u32[]{:S(2)}) %collective-permute-start.1) | collective-permute-done | bytes 163872 | tf_op jit(solution)/shard_map/ppermute | solution.py:239
  13.7 0.7 collective-permute-start.2
  14.4 1.4 %collective-permute-start.8 = (bf16[128,1024]{1,0:T(8,128)(2,1)S(1)}, bf16[128,1024]{1,0:T(8,128)(2,1)S(1)}, u32[]{:S(2)}, u32[]{:S(2)}) collective-permute-start(bf16[128,1024]{1,0:T(8,128)(2,1)S(1)} %pad_maximum_fusion.2._), channel_id=1, source_target_pairs={{0,2},{1,3},{2,0},{3,1},{4,6},{5,7},{6,4},{7,5},{8,10},{9,11},{10,... | collective-permute-start | bytes 786440 | tf_op jit(solution)/shard_map/ppermute | solution.py:239
  15.9 0.7 copy-done.2
  16.5 0.7 copy-done.3
  17.2 0.9 %route_panel.1 = (bf16[512,1024]{1,0:T(8,128)(2,1)S(1)}, f32[64,640]{1,0:T(8,128)S(1)}, bf16[272,1024]{1,0:T(8,128)(2,1)S(1)}, bf16[272,1024]{1,0:T(8,128)(2,1)S(1)}, bf16[544,1024]{1,0:T(8,128)(2,1)S(1)}) custom-call(s32[2]{0:T(128)S(1)} %pad_add_fusion.place_ref, s32[2]{0:T(128)S(1)} %copy-done.2, s32[2]{0:T(128)S(1)} %copy-done.3, ...), custom_call_target="tpu_custom_call" | custom-call | bytes 8388608 | tf_op jit(solution)/shard_map/route_panel/pallas_call | solution.py:328
  18.1 2.7 %collective-permute-done.2 = f32[64,640]{1,0:T(8,128)S(1)} collective-permute-done((f32[64,640]{1,0:T(8,128)S(1)}, f32[64,640]{1,0:T(8,128)S(1)}, u32[]{:S(2)}, u32[]{:S(2)}) %collective-permute-start.2) | collective-permute-done | bytes 163872 | tf_op jit(solution)/shard_map/ppermute | solution.py:239
  20.8 1.5 %collective-permute-start.7 = (f32[64,640]{1,0:T(8,128)S(1)}, f32[64,640]{1,0:T(8,128)S(1)}, u32[]{:S(2)}, u32[]{:S(2)}) collective-permute-start(f32[64,640]{1,0:T(8,128)S(1)} %add.18.refs_3_), channel_id=1, source_target_pairs={{0,1},{1,0},{2,3},{3,2},{4,5},{5,4},{6,7},{7,6},{8,9},{9,8},{10,11... | collective-permute-start | bytes 491528 | tf_op jit(solution)/shard_map/ppermute | solution.py:239
  22.4 0.5 collective-permute-start.13
  22.9 0.5 collective-permute-start.6
  23.4 2.0 %collective-permute-done.8 = bf16[128,1024]{1,0:T(8,128)(2,1)S(1)} collective-permute-done((bf16[128,1024]{1,0:T(8,128)(2,1)S(1)}, bf16[128,1024]{1,0:T(8,128)(2,1)S(1)}, u32[]{:S(2)}, u32[]{:S(2)}) %collective-permute-start.8) | collective-permute-done | bytes 262176 | tf_op jit(solution)/shard_map/ppermute | solution.py:239
  25.4 1.6 %collective-permute-start.5 = (f32[64,640]{1,0:T(8,128)S(1)}, f32[64,640]{1,0:T(8,128)S(1)}, u32[]{:S(2)}, u32[]{:S(2)}) collective-permute-start(f32[64,640]{1,0:T(8,128)S(1)} %collective-permute-done.refs_1_), channel_id=1, source_target_pairs={{0,1},{1,0},{2,3},{3,2},{4,5},{5,4},{6,7},{7,6},{8,9},{9,8},{10,11... | collective-permute-start | bytes 491528 | tf_op jit(solution)/shard_map/ppermute | solution.py:239
  27.0 0.6 collective-permute-start.10
  27.7 2.7 %collective-permute-done.6.refs_6_ = f32[64,640]{1,0:T(8,128)S(1)} collective-permute-done((f32[64,640]{1,0:T(8,128)S(1)}, f32[64,640]{1,0:T(8,128)S(1)}, u32[]{:S(2)}, u32[]{:S(2)}) %collective-permute-start.6) | collective-permute-done | bytes 163872 | tf_op jit(solution)/shard_map/ppermute | solution.py:239
  30.4 2.9 %collective-permute-done.5.refs_5_ = f32[64,640]{1,0:T(8,128)S(1)} collective-permute-done((f32[64,640]{1,0:T(8,128)S(1)}, f32[64,640]{1,0:T(8,128)S(1)}, u32[]{:S(2)}, u32[]{:S(2)}) %collective-permute-start.5) | collective-permute-done | bytes 163872 | tf_op jit(solution)/shard_map/ppermute | solution.py:239
  33.2 0.5 collective-permute-start.16
  33.8 1.5 %collective-permute-start.19 = (bf16[544,1024]{1,0:T(8,128)(2,1)S(1)}, bf16[544,1024]{1,0:T(8,128)(2,1)S(1)}, u32[]{:S(2)}, u32[]{:S(2)}) collective-permute-start(bf16[544,1024]{1,0:T(8,128)(2,1)S(1)} %get-tuple-element.19), channel_id=1, source_target_pairs={{0,16},{8,24},{16,0},{24,8},{1,17},{9,25},{17,1},{25,9},{2,18},{10... | collective-permute-start | bytes 3342344 | tf_op jit(solution)/shard_map/ppermute | solution.py:239
  35.3 2.0 %collective-permute-start.17 = (bf16[256,1024]{1,0:T(8,128)(2,1)S(1)}, bf16[256,1024]{1,0:T(8,128)(2,1)S(1)}, u32[]{:S(2)}, u32[]{:S(2)}) collective-permute-start(bf16[256,1024]{1,0:T(8,128)(2,1)S(1)} %pad_maximum_fusion.1._), channel_id=1, source_target_pairs={{0,4},{1,5},{2,6},{3,7},{4,0},{5,1},{6,2},{7,3},{8,12},{9,13},{10,... | collective-permute-start | bytes 1572872 | tf_op jit(solution)/shard_map/ppermute | solution.py:239
  37.3 30.6 %inverse_factor.1 = (bf16[1024,1024]{1,0:T(8,128)(2,1)S(1)}, bf16[1024,1024]{1,0:T(8,128)(2,1)S(1)}) custom-call(s32[2]{0:T(128)S(1)} %pad_add_fusion.place_ref, f32[64,640]{1,0:T(8,128)S(1)} %fusion.refs_0_, f32[64,640]{1,0:T(8,128)S(1)} %collective-permute-done.refs_1_, f32[64,640]{1,0:T(8,128)S(1)} %collective-permute-done.1.refs_2_, ...), custom_call_target="tpu_custom_call" | custom-call | flops 42949672960 | bytes 8388608 | tf_op jit(solution)/shard_map/inverse_factor/pallas_call | solution.py:219
  68.0 1.6 %solve_top.1.mine_ref = bf16[512,1024]{1,0:T(8,128)(2,1)S(1)} custom-call(bf16[1024,1024]{1,0:T(8,128)(2,1)S(1)} %get-tuple-element.15.hi_ref, bf16[1024,1024]{1,0:T(8,128)(2,1)S(1)} %get-tuple-element.16.lo_ref, bf16[512,1024]{1,0:T(8,128)(2,1)S(1)} %pad_maximum_fusion.x_ref), custom_call_target="tpu_custom_call" | custom-call | flops 1610612736 | bytes 8388608 | tf_op jit(solution)/shard_map/solve_top/pallas_call | solution.py:277
  69.6 0.5 collective-permute-start.20
  70.2 0.1 collective-permute-start.21
  70.4 2.5 %solve_own.1 = bf16[512,1024]{1,0:T(8,128)(2,1)} custom-call(bf16[1024,1024]{1,0:T(8,128)(2,1)S(1)} %get-tuple-element.15.hi_ref, bf16[1024,1024]{1,0:T(8,128)(2,1)S(1)} %get-tuple-element.16.lo_ref, bf16[512,1024]{1,0:T(8,128)(2,1)S(1)} %get-tuple-element.17.x_ref), custom_call_target="tpu_custom_call" | custom-call | flops 1610612736 | bytes 8388608 | tf_op jit(solution)/shard_map/solve_own/pallas_call | solution.py:277
  72.9 0.2 collective-permute-done.20.refs_2_
  73.1 0.8 collective-permute-done.21.refs_3_
  73.9 8.2 %apply_updates.1 = (bf16[128,1024]{1,0:T(8,128)(2,1)}, f32[128,1024]{1,0:T(8,128)}, f32[512,1024]{1,0:T(8,128)}) custom-call(s32[2]{0:T(128)S(1)} %pad_add_fusion.place_ref, bf16[1024,1024]{1,0:T(8,128)(2,1)S(1)} %get-tuple-element.15.hi_ref, bf16[1024,1024]{1,0:T(8,128)(2,1)S(1)} %get-tuple-element.16.lo_ref, bf16[512,1024]{1,0:T(8,128)(2,1)S(1)} %solve_top.1.mine_ref, ...), custom_call_target="tpu_custom_call" | custom-call | flops 5368709120 | bytes 16777216 | tf_op jit(solution)/shard_map/apply_updates/pallas_call | solution.py:405
  (39 shorter events, 0.6 us)
Async XLA Ops:
  0.6 1.0 %copy-start = (f32[128,1024]{1,0:T(8,128)S(1)}, f32[128,1024]{1,0:T(8,128)}, u32[]{:S(2)}) copy-start(f32[128,1024]{1,0:T(8,128)} %param.7) | copy-start | bytes 1572868
  0.6 15.2 %copy-start.1 = (bf16[512,1024]{1,0:T(8,128)(2,1)S(1)}, bf16[512,1024]{1,0:T(8,128)(2,1)}, u32[]{:S(2)}) copy-start(bf16[512,1024]{1,0:T(8,128)(2,1)} %panel_ref.1) | copy-start | bytes 3145732
  1.8 11.9 %collective-permute-start.1 = (f32[64,640]{1,0:T(8,128)S(1)}, f32[64,640]{1,0:T(8,128)S(1)}, u32[]{:S(2)}, u32[]{:S(2)}) collective-permute-start(f32[64,640]{1,0:T(8,128)S(1)} %fusion.refs_0_), channel_id=1, source_target_pairs={{0,4},{1,5},{2,6},{3,7},{4,0},{5,1},{6,2},{7,3},{8,12},{9,13},{10,... | collective-permute-start | bytes 491528 | tf_op jit(solution)/shard_map/ppermute | solution.py:239
  6.8 7.6 %collective-permute-start.3 = (bf16[64,1024]{1,0:T(8,128)(2,1)S(1)}, bf16[64,1024]{1,0:T(8,128)(2,1)S(1)}, u32[]{:S(2)}, u32[]{:S(2)}) collective-permute-start(bf16[64,1024]{1,0:T(8,128)(2,1)S(1)} %constant_dynamic-slice_fusion), channel_id=1, source_target_pairs={{0,1},{1,0},{2,3},{3,2},{4,5},{5,4},{6,7},{7,6},{8,9},{9,8},{10,11... | collective-permute-start | bytes 393224 | tf_op jit(solution)/shard_map/ppermute | solution.py:239
  8.3 14.1 %collective-permute-start.4 = (f32[64,640]{1,0:T(8,128)S(1)}, f32[64,640]{1,0:T(8,128)S(1)}, u32[]{:S(2)}, u32[]{:S(2)}) collective-permute-start(f32[64,640]{1,0:T(8,128)S(1)} %fusion.refs_0_), channel_id=1, source_target_pairs={{0,1},{1,0},{2,3},{3,2},{4,5},{5,4},{6,7},{7,6},{8,9},{9,8},{10,11... | collective-permute-start | bytes 491528 | tf_op jit(solution)/shard_map/ppermute | solution.py:239
  8.9 14.0 %collective-permute-start = (f32[64,640]{1,0:T(8,128)S(1)}, f32[64,640]{1,0:T(8,128)S(1)}, u32[]{:S(2)}, u32[]{:S(2)}) collective-permute-start(f32[64,640]{1,0:T(8,128)S(1)} %fusion.refs_0_), channel_id=1, source_target_pairs={{0,2},{1,3},{2,0},{3,1},{4,6},{5,7},{6,4},{7,5},{8,10},{9,11},{10,... | collective-permute-start | bytes 491528 | tf_op jit(solution)/shard_map/ppermute | solution.py:239
  13.7 7.1 %collective-permute-start.2 = (f32[64,640]{1,0:T(8,128)S(1)}, f32[64,640]{1,0:T(8,128)S(1)}, u32[]{:S(2)}, u32[]{:S(2)}) collective-permute-start(f32[64,640]{1,0:T(8,128)S(1)} %collective-permute-done.1.refs_2_), channel_id=1, source_target_pairs={{0,2},{1,3},{2,0},{3,1},{4,6},{5,7},{6,4},{7,5},{8,10},{9,11},{10,... | collective-permute-start | bytes 491528 | tf_op jit(solution)/shard_map/ppermute | solution.py:239
  14.4 11.0 %collective-permute-start.8 = (bf16[128,1024]{1,0:T(8,128)(2,1)S(1)}, bf16[128,1024]{1,0:T(8,128)(2,1)S(1)}, u32[]{:S(2)}, u32[]{:S(2)}) collective-permute-start(bf16[128,1024]{1,0:T(8,128)(2,1)S(1)} %pad_maximum_fusion.2._), channel_id=1, source_target_pairs={{0,2},{1,3},{2,0},{3,1},{4,6},{5,7},{6,4},{7,5},{8,10},{9,11},{10,... | collective-permute-start | bytes 786440 | tf_op jit(solution)/shard_map/ppermute | solution.py:239
  15.9 0.7 copy-start.2
  16.5 0.7 copy-start.3
  20.8 6.1 %collective-permute-start.7 = (f32[64,640]{1,0:T(8,128)S(1)}, f32[64,640]{1,0:T(8,128)S(1)}, u32[]{:S(2)}, u32[]{:S(2)}) collective-permute-start(f32[64,640]{1,0:T(8,128)S(1)} %add.18.refs_3_), channel_id=1, source_target_pairs={{0,1},{1,0},{2,3},{3,2},{4,5},{5,4},{6,7},{7,6},{8,9},{9,8},{10,11... | collective-permute-start | bytes 491528 | tf_op jit(solution)/shard_map/ppermute | solution.py:239
  22.4 4.6 %collective-permute-start.9 = (f32[64,640]{1,0:T(8,128)S(1)}, f32[64,640]{1,0:T(8,128)S(1)}, u32[]{:S(2)}, u32[]{:S(2)}) collective-permute-start(f32[64,640]{1,0:T(8,128)S(1)} %fusion.refs_0_), channel_id=1, source_target_pairs={{0,8},{8,0},{16,24},{24,16},{1,9},{9,1},{17,25},{25,17},{2,10},{10... | collective-permute-start | bytes 491528 | tf_op jit(solution)/shard_map/ppermute | solution.py:239
  22.4 5.2 %collective-permute-start.13 = (f32[64,640]{1,0:T(8,128)S(1)}, f32[64,640]{1,0:T(8,128)S(1)}, u32[]{:S(2)}, u32[]{:S(2)}) collective-permute-start(f32[64,640]{1,0:T(8,128)S(1)} %collective-permute-done.4.refs_4_), channel_id=1, source_target_pairs={{0,8},{8,0},{16,24},{24,16},{1,9},{9,1},{17,25},{25,17},{2,10},{10... | collective-permute-start | bytes 491528 | tf_op jit(solution)/shard_map/ppermute | solution.py:239
  22.9 7.5 %collective-permute-start.6 = (f32[64,640]{1,0:T(8,128)S(1)}, f32[64,640]{1,0:T(8,128)S(1)}, u32[]{:S(2)}, u32[]{:S(2)}) collective-permute-start(f32[64,640]{1,0:T(8,128)S(1)} %collective-permute-done.1.refs_2_), channel_id=1, source_target_pairs={{0,1},{1,0},{2,3},{3,2},{4,5},{5,4},{6,7},{7,6},{8,9},{9,8},{10,11... | collective-permute-start | bytes 491528 | tf_op jit(solution)/shard_map/ppermute | solution.py:239
  25.4 7.8 %collective-permute-start.5 = (f32[64,640]{1,0:T(8,128)S(1)}, f32[64,640]{1,0:T(8,128)S(1)}, u32[]{:S(2)}, u32[]{:S(2)}) collective-permute-start(f32[64,640]{1,0:T(8,128)S(1)} %collective-permute-done.refs_1_), channel_id=1, source_target_pairs={{0,1},{1,0},{2,3},{3,2},{4,5},{5,4},{6,7},{7,6},{8,9},{9,8},{10,11... | collective-permute-start | bytes 491528 | tf_op jit(solution)/shard_map/ppermute | solution.py:239
  27.0 6.3 %collective-permute-start.11 = (f32[64,640]{1,0:T(8,128)S(1)}, f32[64,640]{1,0:T(8,128)S(1)}, u32[]{:S(2)}, u32[]{:S(2)}) collective-permute-start(f32[64,640]{1,0:T(8,128)S(1)} %collective-permute-done.1.refs_2_), channel_id=1, source_target_pairs={{0,8},{8,0},{16,24},{24,16},{1,9},{9,1},{17,25},{25,17},{2,10},{10... | collective-permute-start | bytes 491528 | tf_op jit(solution)/shard_map/ppermute | solution.py:239
  27.0 6.7 %collective-permute-start.10 = (f32[64,640]{1,0:T(8,128)S(1)}, f32[64,640]{1,0:T(8,128)S(1)}, u32[]{:S(2)}, u32[]{:S(2)}) collective-permute-start(f32[64,640]{1,0:T(8,128)S(1)} %collective-permute-done.refs_1_), channel_id=1, source_target_pairs={{0,8},{8,0},{16,24},{24,16},{1,9},{9,1},{17,25},{25,17},{2,10},{10... | collective-permute-start | bytes 491528 | tf_op jit(solution)/shard_map/ppermute | solution.py:239
  27.6 9.7 %collective-permute-start.12 = (f32[64,640]{1,0:T(8,128)S(1)}, f32[64,640]{1,0:T(8,128)S(1)}, u32[]{:S(2)}, u32[]{:S(2)}) collective-permute-start(f32[64,640]{1,0:T(8,128)S(1)} %add.18.refs_3_), channel_id=1, source_target_pairs={{0,8},{8,0},{16,24},{24,16},{1,9},{9,1},{17,25},{25,17},{2,10},{10... | collective-permute-start | bytes 491528 | tf_op jit(solution)/shard_map/ppermute | solution.py:239
  30.4 4.9 %collective-permute-start.15 = (f32[64,640]{1,0:T(8,128)S(1)}, f32[64,640]{1,0:T(8,128)S(1)}, u32[]{:S(2)}, u32[]{:S(2)}) collective-permute-start(f32[64,640]{1,0:T(8,128)S(1)} %collective-permute-done.6.refs_6_), channel_id=1, source_target_pairs={{0,8},{8,0},{16,24},{24,16},{1,9},{9,1},{17,25},{25,17},{2,10},{10... | collective-permute-start | bytes 491528 | tf_op jit(solution)/shard_map/ppermute | solution.py:239
  33.2 4.0 %collective-permute-start.14 = (f32[64,640]{1,0:T(8,128)S(1)}, f32[64,640]{1,0:T(8,128)S(1)}, u32[]{:S(2)}, u32[]{:S(2)}) collective-permute-start(f32[64,640]{1,0:T(8,128)S(1)} %collective-permute-done.5.refs_5_), channel_id=1, source_target_pairs={{0,8},{8,0},{16,24},{24,16},{1,9},{9,1},{17,25},{25,17},{2,10},{10... | collective-permute-start | bytes 491528 | tf_op jit(solution)/shard_map/ppermute | solution.py:239
  33.2 4.0 %collective-permute-start.16 = (f32[64,640]{1,0:T(8,128)S(1)}, f32[64,640]{1,0:T(8,128)S(1)}, u32[]{:S(2)}, u32[]{:S(2)}) collective-permute-start(f32[64,640]{1,0:T(8,128)S(1)} %hold_piece.1.refs_7_), channel_id=1, source_target_pairs={{0,8},{8,0},{16,24},{24,16},{1,9},{9,1},{17,25},{25,17},{2,10},{10... | collective-permute-start | bytes 491528 | tf_op jit(solution)/shard_map/ppermute | solution.py:239
  33.8 36.4 %collective-permute-start.19 = (bf16[544,1024]{1,0:T(8,128)(2,1)S(1)}, bf16[544,1024]{1,0:T(8,128)(2,1)S(1)}, u32[]{:S(2)}, u32[]{:S(2)}) collective-permute-start(bf16[544,1024]{1,0:T(8,128)(2,1)S(1)} %get-tuple-element.19), channel_id=1, source_target_pairs={{0,16},{8,24},{16,0},{24,8},{1,17},{9,25},{17,1},{25,9},{2,18},{10... | collective-permute-start | bytes 3342344 | tf_op jit(solution)/shard_map/ppermute | solution.py:239
  35.3 32.6 %collective-permute-start.17 = (bf16[256,1024]{1,0:T(8,128)(2,1)S(1)}, bf16[256,1024]{1,0:T(8,128)(2,1)S(1)}, u32[]{:S(2)}, u32[]{:S(2)}) collective-permute-start(bf16[256,1024]{1,0:T(8,128)(2,1)S(1)} %pad_maximum_fusion.1._), channel_id=1, source_target_pairs={{0,4},{1,5},{2,6},{3,7},{4,0},{5,1},{6,2},{7,3},{8,12},{9,13},{10,... | collective-permute-start | bytes 1572872 | tf_op jit(solution)/shard_map/ppermute | solution.py:239
  69.6 4.3 %collective-permute-start.18 = (bf16[512,1024]{1,0:T(8,128)(2,1)S(1)}, bf16[512,1024]{1,0:T(8,128)(2,1)S(1)}, u32[]{:S(2)}, u32[]{:S(2)}) collective-permute-start(bf16[512,1024]{1,0:T(8,128)(2,1)S(1)} %solve_top.1.mine_ref), channel_id=1, source_target_pairs={{0,8},{8,0},{16,24},{24,16},{1,9},{9,1},{17,25},{25,17},{2,10},{10... | collective-permute-start | bytes 3145736 | tf_op jit(solution)/shard_map/ppermute | solution.py:239
  69.6 3.4 %collective-permute-start.20 = (bf16[272,1024]{1,0:T(8,128)(2,1)S(1)}, bf16[272,1024]{1,0:T(8,128)(2,1)S(1)}, u32[]{:S(2)}, u32[]{:S(2)}) collective-permute-start(bf16[272,1024]{1,0:T(8,128)(2,1)S(1)} %get-tuple-element.20), channel_id=1, source_target_pairs={{0,8},{8,0},{16,24},{24,16},{1,9},{9,1},{17,25},{25,17},{2,10},{10... | collective-permute-start | bytes 1671176 | tf_op jit(solution)/shard_map/ppermute | solution.py:239
  70.2 3.7 %collective-permute-start.21 = (bf16[272,1024]{1,0:T(8,128)(2,1)S(1)}, bf16[272,1024]{1,0:T(8,128)(2,1)S(1)}, u32[]{:S(2)}, u32[]{:S(2)}) collective-permute-start(bf16[272,1024]{1,0:T(8,128)(2,1)S(1)} %get-tuple-element.24), channel_id=1, source_target_pairs={{0,8},{8,0},{16,24},{24,16},{1,9},{9,1},{17,25},{25,17},{2,10},{10... | collective-permute-start | bytes 1671176 | tf_op jit(solution)/shard_map/ppermute | solution.py:239
  70.4 3.5 %copy-start.4 = (bf16[512,1024]{1,0:T(8,128)(2,1)S(1)}, bf16[512,1024]{1,0:T(8,128)(2,1)}, u32[]{:S(2)}) copy-start(bf16[512,1024]{1,0:T(8,128)(2,1)} %refs_5_.1) | copy-start | bytes 3145732
  70.4 3.5 %copy-start.5 = (f32[128,1024]{1,0:T(8,128)S(1)}, f32[128,1024]{1,0:T(8,128)}, u32[]{:S(2)}) copy-start(f32[128,1024]{1,0:T(8,128)} %refs_4_.1) | copy-start | bytes 1572868

commit v2 on v1

--- a/solution.py
+++ b/solution.py
@@ -168,7 +168,8 @@
     def solve(k, inverse, columns):
         solved = dot_tn(inverse, right_terms(work[strip(k), columns]))
         work[strip(k), columns] = solved
-        terms[k % 2, :, columns] = both_terms(solved)
+        if k + 1 < count:
+            terms[k % 2, :, columns] = both_terms(solved)
 
     def update(i, k, columns):
         work[strip(i), columns] = work[strip(i), columns] - dot_tn(
@@ -181,7 +182,8 @@
         if k:
             solve(k, inverse, strip(0, k))
         work[strip(k), strip(k)] = plain
-        terms[k % 2, :, strip(k)] = both_terms(plain)
+        if k + 1 < count:
+            terms[k % 2, :, strip(k)] = both_terms(plain)
         upto = (k + 1) * NB
         value = work[strip(k), :upto]
         hi = value.astype(jnp.bfloat16)

time: 82.3 us -> 82.3 us (level)
  no operation moved by 1% of the time
where the time goes in v2:
time: 82.3 us; the launch traced here: 82.1 us
  Pallas kernels  43.8 us (53%)
  starting transfers between devices  19.4 us (24%)
  waiting for transfers between devices  14.5 us (18%)
  local copies, waits for them, and re-layouts  3.34 us (4%)
    pallas_call x1, Pallas kernels, inverse_factor(): pl.pallas_call(kernel, out_shape=(half, half), in_specs=in_specs, out_spe...  30.6 us
    ppermute x22, starting transfers between devices, shifted(): lax.ppermute(x, axis, [(i, i ^ s) for i in range(lax.axis_size(axis))])  19.4 us
    ppermute x22, waiting for transfers between devices, shifted(): lax.ppermute(x, axis, [(i, i ^ s) for i in range(lax.axis_size(axis))])  14.5 us
    pallas_call x1, Pallas kernels, apply_updates(): pl.pallas_call(functools.partial(update_kernel, block_rows), out_shape=(j...  8.23 us
    pallas_call x2, Pallas kernels, solve(): pl.pallas_call(solve_kernel, out_shape=jax.ShapeDtypeStruct(x.shape, jnp....  4.11 us
    unnamed x12, local copies, waits for them, and re-layouts  2.33 us
  transfers between devices with their start and end apart: 22, of which 7 were waited for; matrix products, arithmetic and copies ran while one was open for 1% of the time, Pallas kernels for 43%

profile of v2, /device:TPU:0, one launch (start us, length us, event | category | flops | bytes accessed | tf_op | source)
XLA Modules:
  0.0 82.1 jit_solution(2581747336122994106)
XLA Ops:
  0.7 1.0 %copy-done = f32[128,1024]{1,0:T(8,128)S(1)} copy-done((f32[128,1024]{1,0:T(8,128)S(1)}, f32[128,1024]{1,0:T(8,128)}, u32[]{:S(2)}) %copy-start) | copy-done | bytes 524312
  1.8 4.1 %collective-permute-start.1 = (f32[64,640]{1,0:T(8,128)S(1)}, f32[64,640]{1,0:T(8,128)S(1)}, u32[]{:S(2)}, u32[]{:S(2)}) collective-permute-start(f32[64,640]{1,0:T(8,128)S(1)} %fusion.refs_0_), channel_id=1, source_target_pairs={{0,4},{1,5},{2,6},{3,7},{4,0},{5,1},{6,2},{7,3},{8,12},{9,13},{10,... | collective-permute-start | bytes 491528 | tf_op jit(solution)/shard_map/ppermute | solution.py:241
  5.9 0.9 %constant_dynamic-slice_fusion = bf16[64,1024]{1,0:T(8,128)(2,1)S(1)} fusion(bf16[128,1024]{1,0:T(8,128)(2,1)} %param.8, s32[]{:T(128)S(6)} %select_n.17), kind=kLoop, calls=%fused_computation.6 | loop fusion | bytes 262148 | tf_op jit(solution)/shard_map/dynamic_slice | solution.py:447
  6.8 1.6 %collective-permute-start.3 = (bf16[64,1024]{1,0:T(8,128)(2,1)S(1)}, bf16[64,1024]{1,0:T(8,128)(2,1)S(1)}, u32[]{:S(2)}, u32[]{:S(2)}) collective-permute-start(bf16[64,1024]{1,0:T(8,128)(2,1)S(1)} %constant_dynamic-slice_fusion), channel_id=1, source_target_pairs={{0,1},{1,0},{2,3},{3,2},{4,5},{5,4},{6,7},{7,6},{8,9},{9,8},{10,11... | collective-permute-start | bytes 393224 | tf_op jit(solution)/shard_map/ppermute | solution.py:241
  8.3 0.5 collective-permute-start.4
  8.9 1.6 %collective-permute-start = (f32[64,640]{1,0:T(8,128)S(1)}, f32[64,640]{1,0:T(8,128)S(1)}, u32[]{:S(2)}, u32[]{:S(2)}) collective-permute-start(f32[64,640]{1,0:T(8,128)S(1)} %fusion.refs_0_), channel_id=1, source_target_pairs={{0,2},{1,3},{2,0},{3,1},{4,6},{5,7},{6,4},{7,5},{8,10},{9,11},{10,... | collective-permute-start | bytes 491528 | tf_op jit(solution)/shard_map/ppermute | solution.py:241
  10.4 3.2 %collective-permute-done.1.refs_2_ = f32[64,640]{1,0:T(8,128)S(1)} collective-permute-done((f32[64,640]{1,0:T(8,128)S(1)}, f32[64,640]{1,0:T(8,128)S(1)}, u32[]{:S(2)}, u32[]{:S(2)}) %collective-permute-start.1) | collective-permute-done | bytes 163872 | tf_op jit(solution)/shard_map/ppermute | solution.py:241
  13.7 0.7 collective-permute-start.2
  14.4 1.4 %collective-permute-start.8 = (bf16[128,1024]{1,0:T(8,128)(2,1)S(1)}, bf16[128,1024]{1,0:T(8,128)(2,1)S(1)}, u32[]{:S(2)}, u32[]{:S(2)}) collective-permute-start(bf16[128,1024]{1,0:T(8,128)(2,1)S(1)} %pad_maximum_fusion.2._), channel_id=1, source_target_pairs={{0,2},{1,3},{2,0},{3,1},{4,6},{5,7},{6,4},{7,5},{8,10},{9,11},{10,... | collective-permute-start | bytes 786440 | tf_op jit(solution)/shard_map/ppermute | solution.py:241
  15.9 0.7 copy-done.2
  16.5 0.7 copy-done.3
  17.2 0.9 %route_panel.1 = (bf16[512,1024]{1,0:T(8,128)(2,1)S(1)}, f32[64,640]{1,0:T(8,128)S(1)}, bf16[272,1024]{1,0:T(8,128)(2,1)S(1)}, bf16[272,1024]{1,0:T(8,128)(2,1)S(1)}, bf16[544,1024]{1,0:T(8,128)(2,1)S(1)}) custom-call(s32[2]{0:T(128)S(1)} %pad_add_fusion.place_ref, s32[2]{0:T(128)S(1)} %copy-done.2, s32[2]{0:T(128)S(1)} %copy-done.3, ...), custom_call_target="tpu_custom_call" | custom-call | bytes 8388608 | tf_op jit(solution)/shard_map/route_panel/pallas_call | solution.py:330
  18.1 2.7 %collective-permute-done.2 = f32[64,640]{1,0:T(8,128)S(1)} collective-permute-done((f32[64,640]{1,0:T(8,128)S(1)}, f32[64,640]{1,0:T(8,128)S(1)}, u32[]{:S(2)}, u32[]{:S(2)}) %collective-permute-start.2) | collective-permute-done | bytes 163872 | tf_op jit(solution)/shard_map/ppermute | solution.py:241
  20.8 1.5 %collective-permute-start.7 = (f32[64,640]{1,0:T(8,128)S(1)}, f32[64,640]{1,0:T(8,128)S(1)}, u32[]{:S(2)}, u32[]{:S(2)}) collective-permute-start(f32[64,640]{1,0:T(8,128)S(1)} %add.18.refs_3_), channel_id=1, source_target_pairs={{0,1},{1,0},{2,3},{3,2},{4,5},{5,4},{6,7},{7,6},{8,9},{9,8},{10,11... | collective-permute-start | bytes 491528 | tf_op jit(solution)/shard_map/ppermute | solution.py:241
  22.4 0.5 collective-permute-start.13
  22.9 0.5 collective-permute-start.6
  23.4 2.0 %collective-permute-done.8 = bf16[128,1024]{1,0:T(8,128)(2,1)S(1)} collective-permute-done((bf16[128,1024]{1,0:T(8,128)(2,1)S(1)}, bf16[128,1024]{1,0:T(8,128)(2,1)S(1)}, u32[]{:S(2)}, u32[]{:S(2)}) %collective-permute-start.8) | collective-permute-done | bytes 262176 | tf_op jit(solution)/shard_map/ppermute | solution.py:241
  25.4 1.6 %collective-permute-start.5 = (f32[64,640]{1,0:T(8,128)S(1)}, f32[64,640]{1,0:T(8,128)S(1)}, u32[]{:S(2)}, u32[]{:S(2)}) collective-permute-start(f32[64,640]{1,0:T(8,128)S(1)} %collective-permute-done.refs_1_), channel_id=1, source_target_pairs={{0,1},{1,0},{2,3},{3,2},{4,5},{5,4},{6,7},{7,6},{8,9},{9,8},{10,11... | collective-permute-start | bytes 491528 | tf_op jit(solution)/shard_map/ppermute | solution.py:241
  27.0 0.6 collective-permute-start.10
  27.7 2.7 %collective-permute-done.6.refs_6_ = f32[64,640]{1,0:T(8,128)S(1)} collective-permute-done((f32[64,640]{1,0:T(8,128)S(1)}, f32[64,640]{1,0:T(8,128)S(1)}, u32[]{:S(2)}, u32[]{:S(2)}) %collective-permute-start.6) | collective-permute-done | bytes 163872 | tf_op jit(solution)/shard_map/ppermute | solution.py:241
  30.4 2.9 %collective-permute-done.5.refs_5_ = f32[64,640]{1,0:T(8,128)S(1)} collective-permute-done((f32[64,640]{1,0:T(8,128)S(1)}, f32[64,640]{1,0:T(8,128)S(1)}, u32[]{:S(2)}, u32[]{:S(2)}) %collective-permute-start.5) | collective-permute-done | bytes 163872 | tf_op jit(solution)/shard_map/ppermute | solution.py:241
  33.2 0.5 collective-permute-start.16
  33.8 1.5 %collective-permute-start.19 = (bf16[544,1024]{1,0:T(8,128)(2,1)S(1)}, bf16[544,1024]{1,0:T(8,128)(2,1)S(1)}, u32[]{:S(2)}, u32[]{:S(2)}) collective-permute-start(bf16[544,1024]{1,0:T(8,128)(2,1)S(1)} %get-tuple-element.19), channel_id=1, source_target_pairs={{0,16},{8,24},{16,0},{24,8},{1,17},{9,25},{17,1},{25,9},{2,18},{10... | collective-permute-start | bytes 3342344 | tf_op jit(solution)/shard_map/ppermute | solution.py:241
  35.3 2.0 %collective-permute-start.17 = (bf16[256,1024]{1,0:T(8,128)(2,1)S(1)}, bf16[256,1024]{1,0:T(8,128)(2,1)S(1)}, u32[]{:S(2)}, u32[]{:S(2)}) collective-permute-start(bf16[256,1024]{1,0:T(8,128)(2,1)S(1)} %pad_maximum_fusion.1._), channel_id=1, source_target_pairs={{0,4},{1,5},{2,6},{3,7},{4,0},{5,1},{6,2},{7,3},{8,12},{9,13},{10,... | collective-permute-start | bytes 1572872 | tf_op jit(solution)/shard_map/ppermute | solution.py:241
  37.3 30.6 %inverse_factor.1 = (bf16[1024,1024]{1,0:T(8,128)(2,1)S(1)}, bf16[1024,1024]{1,0:T(8,128)(2,1)S(1)}) custom-call(s32[2]{0:T(128)S(1)} %pad_add_fusion.place_ref, f32[64,640]{1,0:T(8,128)S(1)} %fusion.refs_0_, f32[64,640]{1,0:T(8,128)S(1)} %collective-permute-done.refs_1_, f32[64,640]{1,0:T(8,128)S(1)} %collective-permute-done.1.refs_2_, ...), custom_call_target="tpu_custom_call" | custom-call | flops 42949672960 | bytes 8388608 | tf_op jit(solution)/shard_map/inverse_factor/pallas_call | solution.py:221
  67.9 1.6 %solve_top.1.mine_ref = bf16[512,1024]{1,0:T(8,128)(2,1)S(1)} custom-call(bf16[1024,1024]{1,0:T(8,128)(2,1)S(1)} %get-tuple-element.15.hi_ref, bf16[1024,1024]{1,0:T(8,128)(2,1)S(1)} %get-tuple-element.16.lo_ref, bf16[512,1024]{1,0:T(8,128)(2,1)S(1)} %pad_maximum_fusion.x_ref), custom_call_target="tpu_custom_call" | custom-call | flops 1610612736 | bytes 8388608 | tf_op jit(solution)/shard_map/solve_top/pallas_call | solution.py:279
  69.6 0.5 collective-permute-start.20
  70.2 0.1 collective-permute-start.21
  70.3 2.5 %solve_own.1 = bf16[512,1024]{1,0:T(8,128)(2,1)} custom-call(bf16[1024,1024]{1,0:T(8,128)(2,1)S(1)} %get-tuple-element.15.hi_ref, bf16[1024,1024]{1,0:T(8,128)(2,1)S(1)} %get-tuple-element.16.lo_ref, bf16[512,1024]{1,0:T(8,128)(2,1)S(1)} %get-tuple-element.17.x_ref), custom_call_target="tpu_custom_call" | custom-call | flops 1610612736 | bytes 8388608 | tf_op jit(solution)/shard_map/solve_own/pallas_call | solution.py:279
  72.9 0.2 collective-permute-done.20.refs_2_
  73.0 0.8 collective-permute-done.21.refs_3_
  73.9 8.2 %apply_updates.1 = (bf16[128,1024]{1,0:T(8,128)(2,1)}, f32[128,1024]{1,0:T(8,128)}, f32[512,1024]{1,0:T(8,128)}) custom-call(s32[2]{0:T(128)S(1)} %pad_add_fusion.place_ref, bf16[1024,1024]{1,0:T(8,128)(2,1)S(1)} %get-tuple-element.15.hi_ref, bf16[1024,1024]{1,0:T(8,128)(2,1)S(1)} %get-tuple-element.16.lo_ref, bf16[512,1024]{1,0:T(8,128)(2,1)S(1)} %solve_top.1.mine_ref, ...), custom_call_target="tpu_custom_call" | custom-call | flops 5368709120 | bytes 16777216 | tf_op jit(solution)/shard_map/apply_updates/pallas_call | solution.py:407
  (39 shorter events, 0.6 us)
Async XLA Ops:
  0.6 1.0 %copy-start = (f32[128,1024]{1,0:T(8,128)S(1)}, f32[128,1024]{1,0:T(8,128)}, u32[]{:S(2)}) copy-start(f32[128,1024]{1,0:T(8,128)} %param.7) | copy-start | bytes 1572868
  0.6 15.2 %copy-start.1 = (bf16[512,1024]{1,0:T(8,128)(2,1)S(1)}, bf16[512,1024]{1,0:T(8,128)(2,1)}, u32[]{:S(2)}) copy-start(bf16[512,1024]{1,0:T(8,128)(2,1)} %panel_ref.1) | copy-start | bytes 3145732
  1.8 11.9 %collective-permute-start.1 = (f32[64,640]{1,0:T(8,128)S(1)}, f32[64,640]{1,0:T(8,128)S(1)}, u32[]{:S(2)}, u32[]{:S(2)}) collective-permute-start(f32[64,640]{1,0:T(8,128)S(1)} %fusion.refs_0_), channel_id=1, source_target_pairs={{0,4},{1,5},{2,6},{3,7},{4,0},{5,1},{6,2},{7,3},{8,12},{9,13},{10,... | collective-permute-start | bytes 491528 | tf_op jit(solution)/shard_map/ppermute | solution.py:241
  6.8 7.6 %collective-permute-start.3 = (bf16[64,1024]{1,0:T(8,128)(2,1)S(1)}, bf16[64,1024]{1,0:T(8,128)(2,1)S(1)}, u32[]{:S(2)}, u32[]{:S(2)}) collective-permute-start(bf16[64,1024]{1,0:T(8,128)(2,1)S(1)} %constant_dynamic-slice_fusion), channel_id=1, source_target_pairs={{0,1},{1,0},{2,3},{3,2},{4,5},{5,4},{6,7},{7,6},{8,9},{9,8},{10,11... | collective-permute-start | bytes 393224 | tf_op jit(solution)/shard_map/ppermute | solution.py:241
  8.3 14.1 %collective-permute-start.4 = (f32[64,640]{1,0:T(8,128)S(1)}, f32[64,640]{1,0:T(8,128)S(1)}, u32[]{:S(2)}, u32[]{:S(2)}) collective-permute-start(f32[64,640]{1,0:T(8,128)S(1)} %fusion.refs_0_), channel_id=1, source_target_pairs={{0,1},{1,0},{2,3},{3,2},{4,5},{5,4},{6,7},{7,6},{8,9},{9,8},{10,11... | collective-permute-start | bytes 491528 | tf_op jit(solution)/shard_map/ppermute | solution.py:241
  8.9 14.0 %collective-permute-start = (f32[64,640]{1,0:T(8,128)S(1)}, f32[64,640]{1,0:T(8,128)S(1)}, u32[]{:S(2)}, u32[]{:S(2)}) collective-permute-start(f32[64,640]{1,0:T(8,128)S(1)} %fusion.refs_0_), channel_id=1, source_target_pairs={{0,2},{1,3},{2,0},{3,1},{4,6},{5,7},{6,4},{7,5},{8,10},{9,11},{10,... | collective-permute-start | bytes 491528 | tf_op jit(solution)/shard_map/ppermute | solution.py:241
  13.7 7.1 %collective-permute-start.2 = (f32[64,640]{1,0:T(8,128)S(1)}, f32[64,640]{1,0:T(8,128)S(1)}, u32[]{:S(2)}, u32[]{:S(2)}) collective-permute-start(f32[64,640]{1,0:T(8,128)S(1)} %collective-permute-done.1.refs_2_), channel_id=1, source_target_pairs={{0,2},{1,3},{2,0},{3,1},{4,6},{5,7},{6,4},{7,5},{8,10},{9,11},{10,... | collective-permute-start | bytes 491528 | tf_op jit(solution)/shard_map/ppermute | solution.py:241
  14.4 11.0 %collective-permute-start.8 = (bf16[128,1024]{1,0:T(8,128)(2,1)S(1)}, bf16[128,1024]{1,0:T(8,128)(2,1)S(1)}, u32[]{:S(2)}, u32[]{:S(2)}) collective-permute-start(bf16[128,1024]{1,0:T(8,128)(2,1)S(1)} %pad_maximum_fusion.2._), channel_id=1, source_target_pairs={{0,2},{1,3},{2,0},{3,1},{4,6},{5,7},{6,4},{7,5},{8,10},{9,11},{10,... | collective-permute-start | bytes 786440 | tf_op jit(solution)/shard_map/ppermute | solution.py:241
  15.9 0.7 copy-start.2
  16.5 0.7 copy-start.3
  20.8 6.1 %collective-permute-start.7 = (f32[64,640]{1,0:T(8,128)S(1)}, f32[64,640]{1,0:T(8,128)S(1)}, u32[]{:S(2)}, u32[]{:S(2)}) collective-permute-start(f32[64,640]{1,0:T(8,128)S(1)} %add.18.refs_3_), channel_id=1, source_target_pairs={{0,1},{1,0},{2,3},{3,2},{4,5},{5,4},{6,7},{7,6},{8,9},{9,8},{10,11... | collective-permute-start | bytes 491528 | tf_op jit(solution)/shard_map/ppermute | solution.py:241
  22.4 4.6 %collective-permute-start.9 = (f32[64,640]{1,0:T(8,128)S(1)}, f32[64,640]{1,0:T(8,128)S(1)}, u32[]{:S(2)}, u32[]{:S(2)}) collective-permute-start(f32[64,640]{1,0:T(8,128)S(1)} %fusion.refs_0_), channel_id=1, source_target_pairs={{0,8},{8,0},{16,24},{24,16},{1,9},{9,1},{17,25},{25,17},{2,10},{10... | collective-permute-start | bytes 491528 | tf_op jit(solution)/shard_map/ppermute | solution.py:241
  22.4 5.2 %collective-permute-start.13 = (f32[64,640]{1,0:T(8,128)S(1)}, f32[64,640]{1,0:T(8,128)S(1)}, u32[]{:S(2)}, u32[]{:S(2)}) collective-permute-start(f32[64,640]{1,0:T(8,128)S(1)} %collective-permute-done.4.refs_4_), channel_id=1, source_target_pairs={{0,8},{8,0},{16,24},{24,16},{1,9},{9,1},{17,25},{25,17},{2,10},{10... | collective-permute-start | bytes 491528 | tf_op jit(solution)/shard_map/ppermute | solution.py:241
  22.9 7.5 %collective-permute-start.6 = (f32[64,640]{1,0:T(8,128)S(1)}, f32[64,640]{1,0:T(8,128)S(1)}, u32[]{:S(2)}, u32[]{:S(2)}) collective-permute-start(f32[64,640]{1,0:T(8,128)S(1)} %collective-permute-done.1.refs_2_), channel_id=1, source_target_pairs={{0,1},{1,0},{2,3},{3,2},{4,5},{5,4},{6,7},{7,6},{8,9},{9,8},{10,11... | collective-permute-start | bytes 491528 | tf_op jit(solution)/shard_map/ppermute | solution.py:241
  25.4 7.8 %collective-permute-start.5 = (f32[64,640]{1,0:T(8,128)S(1)}, f32[64,640]{1,0:T(8,128)S(1)}, u32[]{:S(2)}, u32[]{:S(2)}) collective-permute-start(f32[64,640]{1,0:T(8,128)S(1)} %collective-permute-done.refs_1_), channel_id=1, source_target_pairs={{0,1},{1,0},{2,3},{3,2},{4,5},{5,4},{6,7},{7,6},{8,9},{9,8},{10,11... | collective-permute-start | bytes 491528 | tf_op jit(solution)/shard_map/ppermute | solution.py:241
  27.0 6.3 %collective-permute-start.11 = (f32[64,640]{1,0:T(8,128)S(1)}, f32[64,640]{1,0:T(8,128)S(1)}, u32[]{:S(2)}, u32[]{:S(2)}) collective-permute-start(f32[64,640]{1,0:T(8,128)S(1)} %collective-permute-done.1.refs_2_), channel_id=1, source_target_pairs={{0,8},{8,0},{16,24},{24,16},{1,9},{9,1},{17,25},{25,17},{2,10},{10... | collective-permute-start | bytes 491528 | tf_op jit(solution)/shard_map/ppermute | solution.py:241
  27.0 6.7 %collective-permute-start.10 = (f32[64,640]{1,0:T(8,128)S(1)}, f32[64,640]{1,0:T(8,128)S(1)}, u32[]{:S(2)}, u32[]{:S(2)}) collective-permute-start(f32[64,640]{1,0:T(8,128)S(1)} %collective-permute-done.refs_1_), channel_id=1, source_target_pairs={{0,8},{8,0},{16,24},{24,16},{1,9},{9,1},{17,25},{25,17},{2,10},{10... | collective-permute-start | bytes 491528 | tf_op jit(solution)/shard_map/ppermute | solution.py:241
  27.6 9.7 %collective-permute-start.12 = (f32[64,640]{1,0:T(8,128)S(1)}, f32[64,640]{1,0:T(8,128)S(1)}, u32[]{:S(2)}, u32[]{:S(2)}) collective-permute-start(f32[64,640]{1,0:T(8,128)S(1)} %add.18.refs_3_), channel_id=1, source_target_pairs={{0,8},{8,0},{16,24},{24,16},{1,9},{9,1},{17,25},{25,17},{2,10},{10... | collective-permute-start | bytes 491528 | tf_op jit(solution)/shard_map/ppermute | solution.py:241
  30.4 4.9 %collective-permute-start.15 = (f32[64,640]{1,0:T(8,128)S(1)}, f32[64,640]{1,0:T(8,128)S(1)}, u32[]{:S(2)}, u32[]{:S(2)}) collective-permute-start(f32[64,640]{1,0:T(8,128)S(1)} %collective-permute-done.6.refs_6_), channel_id=1, source_target_pairs={{0,8},{8,0},{16,24},{24,16},{1,9},{9,1},{17,25},{25,17},{2,10},{10... | collective-permute-start | bytes 491528 | tf_op jit(solution)/shard_map/ppermute | solution.py:241
  33.2 4.0 %collective-permute-start.14 = (f32[64,640]{1,0:T(8,128)S(1)}, f32[64,640]{1,0:T(8,128)S(1)}, u32[]{:S(2)}, u32[]{:S(2)}) collective-permute-start(f32[64,640]{1,0:T(8,128)S(1)} %collective-permute-done.5.refs_5_), channel_id=1, source_target_pairs={{0,8},{8,0},{16,24},{24,16},{1,9},{9,1},{17,25},{25,17},{2,10},{10... | collective-permute-start | bytes 491528 | tf_op jit(solution)/shard_map/ppermute | solution.py:241
  33.2 4.0 %collective-permute-start.16 = (f32[64,640]{1,0:T(8,128)S(1)}, f32[64,640]{1,0:T(8,128)S(1)}, u32[]{:S(2)}, u32[]{:S(2)}) collective-permute-start(f32[64,640]{1,0:T(8,128)S(1)} %hold_piece.1.refs_7_), channel_id=1, source_target_pairs={{0,8},{8,0},{16,24},{24,16},{1,9},{9,1},{17,25},{25,17},{2,10},{10... | collective-permute-start | bytes 491528 | tf_op jit(solution)/shard_map/ppermute | solution.py:241
  33.8 36.3 %collective-permute-start.19 = (bf16[544,1024]{1,0:T(8,128)(2,1)S(1)}, bf16[544,1024]{1,0:T(8,128)(2,1)S(1)}, u32[]{:S(2)}, u32[]{:S(2)}) collective-permute-start(bf16[544,1024]{1,0:T(8,128)(2,1)S(1)} %get-tuple-element.19), channel_id=1, source_target_pairs={{0,16},{8,24},{16,0},{24,8},{1,17},{9,25},{17,1},{25,9},{2,18},{10... | collective-permute-start | bytes 3342344 | tf_op jit(solution)/shard_map/ppermute | solution.py:241
  35.3 32.6 %collective-permute-start.17 = (bf16[256,1024]{1,0:T(8,128)(2,1)S(1)}, bf16[256,1024]{1,0:T(8,128)(2,1)S(1)}, u32[]{:S(2)}, u32[]{:S(2)}) collective-permute-start(bf16[256,1024]{1,0:T(8,128)(2,1)S(1)} %pad_maximum_fusion.1._), channel_id=1, source_target_pairs={{0,4},{1,5},{2,6},{3,7},{4,0},{5,1},{6,2},{7,3},{8,12},{9,13},{10,... | collective-permute-start | bytes 1572872 | tf_op jit(solution)/shard_map/ppermute | solution.py:241
  69.5 4.3 %collective-permute-start.18 = (bf16[512,1024]{1,0:T(8,128)(2,1)S(1)}, bf16[512,1024]{1,0:T(8,128)(2,1)S(1)}, u32[]{:S(2)}, u32[]{:S(2)}) collective-permute-start(bf16[512,1024]{1,0:T(8,128)(2,1)S(1)} %solve_top.1.mine_ref), channel_id=1, source_target_pairs={{0,8},{8,0},{16,24},{24,16},{1,9},{9,1},{17,25},{25,17},{2,10},{10... | collective-permute-start | bytes 3145736 | tf_op jit(solution)/shard_map/ppermute | solution.py:241
  69.6 3.4 %collective-permute-start.20 = (bf16[272,1024]{1,0:T(8,128)(2,1)S(1)}, bf16[272,1024]{1,0:T(8,128)(2,1)S(1)}, u32[]{:S(2)}, u32[]{:S(2)}) collective-permute-start(bf16[272,1024]{1,0:T(8,128)(2,1)S(1)} %get-tuple-element.20), channel_id=1, source_target_pairs={{0,8},{8,0},{16,24},{24,16},{1,9},{9,1},{17,25},{25,17},{2,10},{10... | collective-permute-start | bytes 1671176 | tf_op jit(solution)/shard_map/ppermute | solution.py:241
  70.2 3.7 %collective-permute-start.21 = (bf16[272,1024]{1,0:T(8,128)(2,1)S(1)}, bf16[272,1024]{1,0:T(8,128)(2,1)S(1)}, u32[]{:S(2)}, u32[]{:S(2)}) collective-permute-start(bf16[272,1024]{1,0:T(8,128)(2,1)S(1)} %get-tuple-element.24), channel_id=1, source_target_pairs={{0,8},{8,0},{16,24},{24,16},{1,9},{9,1},{17,25},{25,17},{2,10},{10... | collective-permute-start | bytes 1671176 | tf_op jit(solution)/shard_map/ppermute | solution.py:241
  70.3 3.5 %copy-start.4 = (bf16[512,1024]{1,0:T(8,128)(2,1)S(1)}, bf16[512,1024]{1,0:T(8,128)(2,1)}, u32[]{:S(2)}) copy-start(bf16[512,1024]{1,0:T(8,128)(2,1)} %refs_5_.1) | copy-start | bytes 3145732
  70.3 3.5 %copy-start.5 = (f32[128,1024]{1,0:T(8,128)S(1)}, f32[128,1024]{1,0:T(8,128)}, u32[]{:S(2)}) copy-start(f32[128,1024]{1,0:T(8,128)} %refs_4_.1) | copy-start | bytes 1572868
